TPU v7x, 32 devices: a whole 2x2x4 slice. The times are simulated.
32 devices in a mesh: member: 4 (over z), row: 8 (over y, x, core).
Axes of the slice: x: 2, y: 2, z: 4, core: 2. Of those that a mesh axis runs over, the one named last changes fastest.
Arguments:
- action: bfloat16 [2048, 1024], P('row'), may hold values from -6 to 6
- state_term: bfloat16 [8, 2048, 4096], P('member', 'row'), may hold values from -6 to 6
- target: float32 [2048], P('row'), may hold values from -6 to 6
- weight_a: bfloat16 [8, 1024, 4096], P('member', 'row'), may hold values from -0.21875 to 0.21875
- value_w: bfloat16 [8, 4096], P('member'), may hold values from -0.0234375 to 0.0234375
Outputs:
- weight_grad: bfloat16 [8, 1024, 4096], P('member', 'row')
- value_grad: float32 [8, 4096], P('member')
- state_grad: bfloat16 [8, 2048, 4096], P('member', 'row')
- diversity: float32 [2048], P('row')
All inputs are finite; a program needn't handle non-finite values.
Results may differ from a plain program's by a relative error of at most 0.03.
Values may be sent and summed in bfloat16 or wider, within the bound.
No kernel may reach another device: no remote copies, remote signals or barrier semaphores. Data moves between devices by JAX's collectives and lax.ppermute only.
A program may use at most 128 MiB of HBM per device.

v0:
```python
import jax
import jax.numpy as jnp
from jax import lax
from jax.sharding import PartitionSpec as P

EPS = 1e-06
ETA = 5.0


def forward_member(weights, value_row, state_rows, action):
    pre_act = state_rows.astype(jnp.float32) + jnp.dot(
        action, weights, preferred_element_type=jnp.float32
    )
    sigmoid_part = jax.nn.sigmoid(pre_act)
    hidden = pre_act * sigmoid_part
    slope_first = sigmoid_part * (1.0 + pre_act * (1.0 - sigmoid_part))
    slope_second = (
        sigmoid_part * (1.0 - sigmoid_part) * (2.0 + pre_act * (1.0 - 2.0 * sigmoid_part))
    )
    value_float = value_row.astype(jnp.float32)
    q_value = jnp.sum(hidden * value_float, axis=-1)
    tangent = (slope_first * value_float).astype(jnp.bfloat16)
    action_grad = lax.dot_general(
        tangent, weights, (((1,), (1,)), ((), ())), preferred_element_type=jnp.float32
    )
    grad_norm = jnp.sqrt(jnp.sum(action_grad * action_grad, axis=-1, keepdims=True) + EPS)
    unit_grad = action_grad / grad_norm
    return (hidden, slope_first, slope_second, q_value, tangent, unit_grad, grad_norm)


def weight_term(left, right):
    return lax.dot_general(
        left, right, (((0,), (0,)), ((), ())), preferred_element_type=jnp.float32
    )


def body(action, state_term, target, weight_a, value_w):
    members = weight_a.shape[0]
    pairs = members * lax.axis_size("member") * (members * lax.axis_size("member") - 1)
    stored = []
    for member_pos in range(members):
        gathered = lax.all_gather(weight_a[member_pos], "row", axis=0, tiled=True)
        results = forward_member(gathered, value_w[member_pos], state_term[member_pos], action)
        stored.append((gathered,) + results)
    unit_stack = jnp.stack([entry[6].astype(jnp.bfloat16) for entry in stored], axis=0)
    everyone = lax.all_gather(unit_stack, "member", axis=0, tiled=True)
    total = jnp.sum(everyone.astype(jnp.float32), axis=0)
    gram = jnp.einsum("mra,nra->rmn", everyone, everyone, preferred_element_type=jnp.float32)
    diagonal_sum = jnp.trace(gram, axis1=1, axis2=2)
    diversity = (jnp.sum(gram, axis=(1, 2)) - diagonal_sum) / pairs
    weight_grads = []
    value_grads = []
    state_grads = []
    for member_pos in range(members):
        weights, hidden, slope_first, slope_second, q_value, tangent, unit_grad, grad_norm = stored[
            member_pos
        ]
        dir_grad = 2.0 * ETA / pairs * (total - unit_stack[member_pos].astype(jnp.float32))
        along = jnp.sum(unit_grad * dir_grad, axis=-1, keepdims=True)
        cotangent = ((dir_grad - unit_grad * along) / grad_norm).astype(jnp.bfloat16)
        back_term = jnp.dot(cotangent, weights, preferred_element_type=jnp.float32)
        residue = (q_value - target)[:, None]
        value_float = value_w[member_pos].astype(jnp.float32)
        pre_grad = value_float * (slope_first * residue + slope_second * back_term)
        value_grads.append(jnp.sum(hidden * residue + slope_first * back_term, axis=0))
        pre_b = pre_grad.astype(jnp.bfloat16)
        state_grads.append(pre_b)
        left = jnp.concatenate([action, cotangent], axis=0)
        right = jnp.concatenate([pre_b, tangent], axis=0)
        summed = lax.psum_scatter(
            weight_term(left, right).astype(jnp.bfloat16), "row", scatter_dimension=0, tiled=True
        )
        weight_grads.append(summed)
    value_total = lax.psum(jnp.stack(value_grads, axis=0).astype(jnp.bfloat16), "row").astype(
        jnp.float32
    )
    return (jnp.stack(weight_grads, axis=0), value_total, jnp.stack(state_grads, axis=0), diversity)


def solution(mesh):
    in_specs = (
        P("row", None),
        P("member", "row", None),
        P("row"),
        P("member", "row", None),
        P("member", None),
    )
    out_specs = (P("member", "row", None), P("member", None), P("member", "row", None), P("row"))
    return jax.shard_map(body, mesh=mesh, in_specs=in_specs, out_specs=out_specs, check_vma=False)
```

profile of v0, /device:TPU:0, one launch (start us, length us, event | category | flops | bytes accessed | tf_op | source)
XLA Modules:
  0.0 393.0 jit_solution(9429809490590834874)
XLA Ops:
  7.2 3.1 fusion.46
  10.4 0.0 all-gather.8.cloned.1.call-start
  10.4 0.7 all-gather.8.cloned.1.call-update
  11.1 0.0 all-gather.6.cloned.1.call-start
  11.2 56.4 %all-gather.10.cloned.1.call-done = bf16[1,1024,4096]{2,1,0:T(8,128)(2,1)} async-done(((bf16[1,128,4096]{2,1,0:T(8,128)(2,1)}), bf16[1,1024,4096]{2,1,0:T(8,128)(2,1)}) %all-gather.10.cloned.1.call-update) | async-done | bytes 8388624 | tf_op jit(solution)/shard_map/all_gather | solution.py:42
  67.6 9.7 %multiply_reduce_fusion = (f32[256]{0:T(256)S(1)}, bf16[256,4096]{1,0:T(8,128)(2,1)S(1)}, f32[256,4096]{1,0:T(8,128)}) fusion(f32[4096]{0:T(1024)S(1)} %bitcast.58, bf16[256,1024]{1,0:T(8,128)(2,1)S(1)} %copy-done.6, bf16[1,1024,4096]{2,1,0:T(8,128)(2,1)} %all-gather.10.cloned.1.call-done, bf16[2,256,4096]{2,1,0:T(8,128)(2,1)} %param.6), kind=kOutput, calls=%fused_computation.46 | convolution fusion | flops 2162163456 | bytes 17318912 | tf_op jit(solution)/shard_map/dot_general | solution.py:11
  77.4 2.7 multiply_reduce_fusion.4
  80.1 43.9 %all-gather.8.cloned.1.call-done = bf16[1,1024,4096]{2,1,0:T(8,128)(2,1)} async-done(((bf16[1,128,4096]{2,1,0:T(8,128)(2,1)}), bf16[1,1024,4096]{2,1,0:T(8,128)(2,1)}) %all-gather.8.cloned.1.call-update) | async-done | bytes 8388624 | tf_op jit(solution)/shard_map/all_gather | solution.py:42
  124.0 9.7 %multiply_reduce_fusion.1 = (f32[256]{0:T(256)S(1)}, bf16[256,4096]{1,0:T(8,128)(2,1)S(1)}, f32[256,4096]{1,0:T(8,128)}) fusion(f32[4096]{0:T(1024)S(1)} %bitcast.56, bf16[256,1024]{1,0:T(8,128)(2,1)S(1)} %copy-done.6, bf16[1,1024,4096]{2,1,0:T(8,128)(2,1)} %all-gather.8.cloned.1.call-done, bf16[2,256,4096]{2,1,0:T(8,128)(2,1)} %param.6), kind=kOutput, calls=%fused_computation.47 | convolution fusion | flops 2162163456 | bytes 17318912 | tf_op jit(solution)/shard_map/dot_general | solution.py:11
  133.7 2.4 multiply_reduce_fusion.5
  136.2 0.3 convert_bitcast_fusion
  136.5 1.1 pad_maximum_fusion.6
  137.6 0.2 reduce-scatter.5.cloned.1.call-start
  137.8 80.7 %all-gather.6.cloned.1.call-done = bf16[8,256,1024]{2,1,0:T(8,128)(2,1)} async-done(((bf16[2,256,1024]{2,1,0:T(8,128)(2,1)}), bf16[8,256,1024]{2,1,0:T(8,128)(2,1)}) %all-gather.6.cloned.1.call-update) | async-done | bytes 4194320 | tf_op jit(solution)/shard_map/all_gather | solution.py:46
  218.5 3.2 convert_reduce_fusion
  221.7 0.5 multiply_reduce_fusion.3
  222.2 0.5 divide_convert_fusion.1
  222.8 1.1 copy-done.11
  223.9 7.4 %add_reduce_fusion = (bf16[4096]{0:T(1024)(128)(2,1)S(1)}, bf16[256,4096]{1,0:T(8,128)(2,1)S(1)}) fusion(f32[256]{0:T(256)S(1)} %get-tuple-element.23, f32[256,4096]{1,0:T(8,128)S(1)} %copy-done.11, f32[4096]{0:T(1024)S(1)} %bitcast.59, bf16[256,1024]{1,0:T(8,128)(2,1)S(1)} %get-tuple-element.19, bf16[1,1024,4096]{2,1,0:T(8,128)(2,1)} %all-gather.10.cloned.1.call-done), kind=kOutput, calls=%fused_computation.44 | convolution fusion | flops 2171596800 | bytes 15229952 | tf_op jit(solution)/shard_map/dot_general | solution.py:61
  231.3 6.8 %convolution_convert_fusion = bf16[1024,4096]{1,0:T(8,128)(2,1)} fusion(bf16[256,4096]{1,0:T(8,128)(2,1)S(1)} %copy-done.10, bf16[256,4096]{1,0:T(8,128)(2,1)S(1)} %get-tuple-element.11, bf16[256,1024]{1,0:T(8,128)(2,1)S(1)} %copy-done.6, bf16[256,1024]{1,0:T(8,128)(2,1)S(1)} %get-tuple-element.19), kind=kOutput, calls=%fused_computation.13 | convolution fusion | flops 4309647360 | bytes 13631488 | tf_op jit(solution)/shard_map/dot_general | solution.py:32
  238.1 0.0 reduce-scatter.3.cloned.1.call-start
  238.2 10.2 %add_reduce_fusion.1 = (bf16[4096]{0:T(1024)(128)(2,1)S(1)}, bf16[256,4096]{1,0:T(8,128)(2,1)S(1)}) fusion(f32[256]{0:T(256)S(1)} %get-tuple-element.22, f32[256,4096]{1,0:T(8,128)} %get-tuple-element.27, f32[4096]{0:T(1024)S(1)} %bitcast.57, bf16[256,1024]{1,0:T(8,128)(2,1)S(1)} %get-tuple-element.18, bf16[1,1024,4096]{2,1,0:T(8,128)(2,1)} %all-gather.8.cloned.1.call-done), kind=kOutput, calls=%fused_computation.45 | convolution fusion | flops 2171596800 | bytes 15229952 | tf_op jit(solution)/shard_map/dot_general | solution.py:61
  248.5 1.3 copy-done
  249.8 6.8 %convolution_convert_fusion.1 = bf16[1024,4096]{1,0:T(8,128)(2,1)} fusion(bf16[256,4096]{1,0:T(8,128)(2,1)S(1)} %copy-done.8, bf16[256,4096]{1,0:T(8,128)(2,1)S(1)} %get-tuple-element.9, bf16[256,1024]{1,0:T(8,128)(2,1)S(1)} %copy-done.6, bf16[256,1024]{1,0:T(8,128)(2,1)S(1)} %get-tuple-element.18), kind=kOutput, calls=%fused_computation.14 | convolution fusion | flops 4309647360 | bytes 13631488 | tf_op jit(solution)/shard_map/dot_general | solution.py:32
  256.7 24.6 %psum.7 = bf16[2,4096]{1,0:T(2,128)(2,1)S(1)} all-reduce(bf16[2,4096]{1,0:T(2,128)(2,1)S(1)} %pad_maximum_fusion.7), channel_id=1, replica_groups=mesh['member'=4,'row'=8] {'row'}, use_global_device_ids=true, to_apply=%region_11.12 | all-reduce | flops 8192 | bytes 32768 | tf_op jit(solution)/shard_map/psum | solution.py:74
  281.3 0.6 convert_element_type.78
  281.9 8.8 %select_reduce_fusion = (f32[256]{0:T(256)S(1)}, f32[256]{0:T(256)S(1)}) fusion(pred[8,8]{1,0:T(8,128)(4,1)S(1)} %iota_compare_fusion, bf16[8,256,1024]{2,1,0:T(8,128)(2,1)} %all-gather.6.cloned.1.call-done), kind=kOutput, calls=%fused_computation.60 | convolution fusion | flops 33603072 | bytes 4196416 | tf_op jit(solution)/shard_map/mra,nra->rmn/dot_general | solution.py:48
  290.7 0.6 subtract_multiply_fusion.6
  291.3 2.4 pad_maximum_fusion
  293.7 14.7 %reduce-scatter.5.cloned.1.call-done = bf16[128,4096]{1,0:T(8,128)(2,1)} async-done(((bf16[1024,4096]{1,0:T(8,128)(2,1)}), bf16[128,4096]{1,0:T(8,128)(2,1)}) %reduce-scatter.5.cloned.1.call-update) | async-done | bytes 1048592 | tf_op jit(solution)/shard_map/reduce_scatter | solution.py:70
  308.4 75.0 %reduce-scatter.3.cloned.1.call-done = bf16[128,4096]{1,0:T(8,128)(2,1)} async-done(((bf16[1024,4096]{1,0:T(8,128)(2,1)}), bf16[128,4096]{1,0:T(8,128)(2,1)}) %reduce-scatter.3.cloned.1.call-update) | async-done | bytes 1048592 | tf_op jit(solution)/shard_map/reduce_scatter | solution.py:70
  383.4 3.1 pad_maximum_fusion.1
  (35 shorter events, 0.3 us)
Async XLA Ops:
  7.2 4.0 %copy-start.2 = (bf16[2,4096]{1,0:T(2,128)(2,1)S(1)}, bf16[2,4096]{1,0:T(2,128)(2,1)}, u32[]{:S(2)}) copy-start(bf16[2,4096]{1,0:T(2,128)(2,1)} %param.9) | copy-start | bytes 49156
  7.2 60.5 %copy-start.6 = (bf16[256,1024]{1,0:T(8,128)(2,1)S(1)}, bf16[256,1024]{1,0:T(8,128)(2,1)}, u32[]{:S(2)}) copy-start(bf16[256,1024]{1,0:T(8,128)(2,1)} %param.5) | copy-start | bytes 1572868
  7.2 60.4 %all-gather.10.cloned.1.call-start = ((), (), s32[]{:S(2)}) async-start(), calls=%async_computation.6 | async-start | bytes 9437184 | tf_op jit(solution)/shard_map/all_gather | solution.py:42
  10.4 113.6 %all-gather.8.cloned.1.call-start = ((), (), s32[]{:S(2)}) async-start(), calls=%async_computation.5 | async-start | bytes 9437184 | tf_op jit(solution)/shard_map/all_gather | solution.py:42
  11.1 207.4 %all-gather.6.cloned.1.call-start = ((), (), s32[]{:S(2)}) async-start(), calls=%async_computation.2 | async-start | bytes 5242880 | tf_op jit(solution)/shard_map/all_gather | solution.py:46
  67.6 9.7 %copy-start.5 = (bf16[1,1024,4096]{2,1,0:T(8,128)(2,1)S(1)}, bf16[1,1024,4096]{2,1,0:T(8,128)(2,1)}, u32[]{:S(2)}) copy-start(bf16[1,1024,4096]{2,1,0:T(8,128)(2,1)} %all-gather.10.cloned.1.call-done) | copy-start | bytes 25165828
  77.4 2.7 copy-start.9
  124.0 9.8 %copy-start.4 = (bf16[1,1024,4096]{2,1,0:T(8,128)(2,1)S(1)}, bf16[1,1024,4096]{2,1,0:T(8,128)(2,1)}, u32[]{:S(2)}) copy-start(bf16[1,1024,4096]{2,1,0:T(8,128)(2,1)} %all-gather.8.cloned.1.call-done) | copy-start | bytes 25165828
  133.7 2.4 copy-start.7
  136.2 1.6 copy-start.3
  137.6 170.8 %reduce-scatter.5.cloned.1.call-start = ((), (), s32[]{:S(2)}) async-start(), calls=%async_computation.4 | async-start | bytes 9437184 | tf_op jit(solution)/shard_map/reduce_scatter | solution.py:70
  221.7 2.2 copy-start.11
  223.9 7.4 %copy-start.10 = (bf16[256,4096]{1,0:T(8,128)(2,1)S(1)}, bf16[256,4096]{1,0:T(8,128)(2,1)}, u32[]{:S(2)}) copy-start(bf16[256,4096]{1,0:T(8,128)(2,1)} %copy-done.9) | copy-start | bytes 6291460
  238.1 145.3 %reduce-scatter.3.cloned.1.call-start = ((), (), s32[]{:S(2)}) async-start(), calls=%async_computation.3 | async-start | bytes 9437184 | tf_op jit(solution)/shard_map/reduce_scatter | solution.py:70
  238.2 11.6 %copy-start.8 = (bf16[256,4096]{1,0:T(8,128)(2,1)S(1)}, bf16[256,4096]{1,0:T(8,128)(2,1)}, u32[]{:S(2)}) copy-start(bf16[256,4096]{1,0:T(8,128)(2,1)} %copy-done.7) | copy-start | bytes 6291460
  248.4 1.3 copy-start
  281.9 9.4 %copy-start.1 = (bf16[256,4096]{1,0:T(8,128)(2,1)S(1)}, bf16[256,4096]{1,0:T(8,128)(2,1)}, u32[]{:S(2)}) copy-start(bf16[256,4096]{1,0:T(8,128)(2,1)} %copy-done) | copy-start | bytes 6291460
Sparse Core Ops, SparseCore 0:
  10.5 57.0 all-gather.9
  69.5 54.3 all-gather.7
  137.7 80.7 all-gather.5
  238.3 70.0 reduce-scatter.4
  312.1 71.2 reduce-scatter.2
where the time goes:
time: 393 us
  waiting for transfers between devices  271 us (69%)
  matrix products  64.7 us (16%)
  blocking collectives  24.6 us (6%)
  between operations  14 us (4%)
  other arithmetic  12.3 us (3%)
  local copies, waits for them, and re-layouts  5.6 us (1%)
    all_gather x2, waiting for transfers between devices, body(): gathered = lax.all_gather(weight_a[member_pos], 'row', axis=0, tiled=True)  100 us
    reduce_scatter x2, waiting for transfers between devices, body(): lax.psum_scatter(weight_term(left, right).astype(jnp.bfloat16), 'row', sc...  89.7 us
    all_gather x1, waiting for transfers between devices, body(): everyone = lax.all_gather(unit_stack, 'member', axis=0, tiled=True)  80.7 us
    psum x1, blocking collectives, body(): lax.psum(jnp.stack(value_grads, axis=0).astype(jnp.bfloat16), 'row')  24.6 us
    dot_general x2, matrix products, forward_member(): jnp.dot(action, weights, preferred_element_type=jnp.float32)  19.5 us
    dot_general x2, matrix products, body(): back_term = jnp.dot(cotangent, weights, preferred_element_type=jnp.float32)  17.6 us
    dot_general x2, matrix products, weight_term(): lax.dot_general(left, right, (((0,), (0,)), ((), ())), preferred_element_...  13.6 us
    dot_general x1, matrix products, body(): jnp.einsum('mra,nra->rmn', everyone, everyone, preferred_element_type=jnp...  8.84 us
  transfers between devices with their start and end apart: 5, of which 5 were waited for; matrix products, arithmetic and copies ran while one was open for 11% of the time, Pallas kernels for 0%

commit v1 on v0

v1 whole, which is shorter than its diff:
```python
import functools

import jax
import jax.numpy as jnp
from jax import lax
from jax.experimental import pallas as pl
from jax.experimental.pallas import tpu as pltpu
from jax.sharding import PartitionSpec as P

EPS = 1e-06
ETA = 5.0
UNIT = 512
GATHER_CUTS = ((4, 4), (4, 2, 2))
SCATTER_CUTS = ((1, 1, 2, 4), (4, 2, 2))
TILE = 512
STRIP = 16
F32 = jnp.float32
BF16 = jnp.bfloat16
PARAMS = dict(vmem_limit_bytes=16 * 1024 * 1024)
LIGHT = pl.CostEstimate(flops=1000000, bytes_accessed=100000, transcendentals=0)


def tie(x, *earlier):
    return lax.optimization_barrier((x,) + earlier)[0]


def in_hbm(xs):
    return [pltpu.with_memory_space_constraint(x, pltpu.HBM) for x in xs]


def plan(cuts, held, width):
    out = []
    for m in range(held):
        lo = 0
        for units in cuts[0] if m < held - 1 else cuts[1]:
            out.append((m, lo, units * UNIT))
            lo += units * UNIT
        assert lo == width
    return out


class Ring:
    def __init__(self, n_row):
        self.n_row = n_row
        self.chips = n_row // 2
        self.half = self.chips // 2
        order = list(range(self.half)) + [self.chips + self.half - 1 - p for p in range(self.half, self.chips)]
        up, down, swap = [], [], []
        for pos in range(self.chips):
            for core in range(2):
                here = order[pos] * 2 + core
                step = 1 - 2 * core
                up.append((here, order[(pos + step) % self.chips] * 2 + core))
                down.append((here, order[(pos - step) % self.chips] * 2 + core))
                swap.append((here, order[pos] * 2 + 1 - core))
        self.up, self.down, self.swap = up, down, swap

    def onward(self, x):
        return lax.ppermute(x, "row", self.up)

    def backward(self, x):
        return lax.ppermute(x, "row", self.down)

    def partner(self, x):
        return lax.ppermute(x, "row", self.swap)

    def blocks(self):
        me = lax.axis_index("row")
        chip, core = me // 2, me % 2
        flip = self.chips + self.half - 1
        pos = jnp.where(chip < self.half, chip, flip - chip)

        def index(p, c):
            p = (p + 2 * self.chips) % self.chips
            return jnp.where(p < self.half, p, flip - p) * 2 + c

        out = []
        for c, step in ((core, 1 - 2 * core), (1 - core, 2 * core - 1)):
            out.append(index(pos, c))
            for t in range(1, self.half):
                out.append(index(pos - step * t, c))
                out.append(index(pos - step * t, 1 - c))
            out.append(index(pos - step * self.half, c))
        return jnp.stack(out).astype(jnp.int32)


def slopes(pre):
    turn = jnp.tanh(0.5 * pre)
    sig = 0.5 * turn + 0.5
    rest = 1.0 - sig
    spread = sig * rest
    one = sig + pre * spread
    two = spread * (2.0 - pre * turn)
    return pre * sig, one, two


def inverse_norm(g):
    return 1.0 / jnp.sqrt(jnp.sum(g * g, axis=-1, keepdims=True) + EPS)


def full(shape):
    return pl.BlockSpec(shape, lambda *_: (0,) * len(shape))


def permute_action(action, blocks):
    rows, width = action.shape
    count = blocks.shape[0]
    size = width // count
    if size % 128:
        moved = jnp.take(action.reshape(rows, count, size), blocks, axis=1).reshape(rows, width)
        return moved, moved.T

    def kernel(idx_ref, x_ref, out_ref, turned_ref):
        x = x_ref[...]
        out_ref[...] = x
        turned_ref[...] = x.astype(F32).T.astype(BF16)

    return pl.pallas_call(
        kernel,
        grid_spec=pltpu.PrefetchScalarGridSpec(
            num_scalar_prefetch=1,
            grid=(count,),
            in_specs=[pl.BlockSpec((rows, size), lambda j, idx: (0, idx[j]))],
            out_specs=[
                pl.BlockSpec((rows, size), lambda j, idx: (0, j)),
                pl.BlockSpec((size, rows), lambda j, idx: (j, 0)),
            ],
        ),
        out_shape=[
            jax.ShapeDtypeStruct((rows, width), BF16),
            jax.ShapeDtypeStruct((width, rows), BF16),
        ],
        compiler_params=pltpu.CompilerParams(**PARAMS),
        cost_estimate=LIGHT,
        name="permute_action",
    )(blocks, action)


def front(member, lo, action, state, weight_a, pieces, value_w, carry):
    rows, width = action.shape
    size, cols = pieces[0].shape
    tile = min(TILE, cols)
    steps = cols // tile
    base = lo // tile
    held = weight_a.shape[0]
    n_in = 4 + len(pieces)

    def kernel(*refs):
        action_ref, state_ref, own_ref, value_ref = refs[:4]
        rest = refs[4:n_in]
        pre_ref, q_ref, g_ref = refs[-3:]

        @pl.when(pl.program_id(0) == 0)
        def _():
            if carry is None:
                q_ref[...] = jnp.zeros_like(q_ref)
                g_ref[...] = jnp.zeros_like(g_ref)
            else:
                q_ref[...] = refs[n_in][...]
                g_ref[...] = refs[n_in + 1][...]

        weights = jnp.concatenate([own_ref[0]] + [r[...] for r in rest], axis=0)
        pre_ref[...] = jnp.dot(action_ref[...], weights, preferred_element_type=F32)
        value = value_ref[pl.ds(member, 1), :].astype(F32)
        tangents = []
        for r in range(0, rows, STRIP):
            cut = pl.ds(r, STRIP)
            pre = pre_ref[cut, :] + state_ref[0, cut, :].astype(F32)
            pre_ref[cut, :] = pre
            hidden, one, _ = slopes(pre)
            prod = hidden * value
            lanes = prod[:, :128]
            for c in range(128, tile, 128):
                lanes = lanes + prod[:, c : c + 128]
            q_ref[cut, :] += lanes
            tangents.append((one * value).astype(BF16))
        tangent = jnp.concatenate(tangents, axis=0)
        g_ref[...] += lax.dot_general(
            tangent, weights, (((1,), (1,)), ((), ())), preferred_element_type=F32
        )

    piece = pl.BlockSpec((size, tile), lambda j: (0, j))
    in_specs = [
        full((rows, width)),
        pl.BlockSpec((1, rows, tile), lambda j: (member, 0, base + j)),
        pl.BlockSpec((1, size, tile), lambda j: (member, 0, base + j)),
        pl.BlockSpec((held, tile), lambda j: (0, base + j)),
    ] + [piece] * len(pieces)
    args = [action, state, weight_a, value_w] + list(pieces)
    aliases = {}
    if carry is not None:
        in_specs += [full((rows, 128)), full((rows, width))]
        args += list(carry)
        aliases = {n_in: 1, n_in + 1: 2}
    return pl.pallas_call(
        kernel,
        grid=(steps,),
        in_specs=in_specs,
        out_specs=[pl.BlockSpec((rows, tile), lambda j: (0, j)), full((rows, 128)), full((rows, width))],
        out_shape=[
            pltpu.HBM((rows, cols), F32),
            pltpu.HBM((rows, 128), F32),
            pltpu.HBM((rows, width), F32),
        ],
        input_output_aliases=aliases,
        compiler_params=pltpu.CompilerParams(**PARAMS),
        cost_estimate=LIGHT,
        name="front",
    )(*in_hbm(args[:4]), *args[4:])


def unit_sums(bit, grads):
    rows, width = grads[0].shape
    half = rows // 2
    part = half // 2
    count = len(grads)

    def kernel(bit_ref, *refs):
        keeps, sends, square_ref = refs[count : count + 2], refs[count + 2 : count + 4], refs[count + 4]
        total = jnp.zeros((half, width), F32)
        square = jnp.zeros((half, 1), F32)
        for g_ref in refs[:count]:
            g = g_ref[...]
            unit = (g * inverse_norm(g)).astype(BF16).astype(F32)
            total = total + unit
            square = square + jnp.sum(unit * unit, axis=-1, keepdims=True)
        square_ref[...] = square
        step = pl.program_id(0)

        @pl.when(step == 0)
        def _():
            for i, ref in enumerate(sends):
                ref[...] = total[i * part : (i + 1) * part].astype(BF16)

        @pl.when(step == 1)
        def _():
            for i, ref in enumerate(keeps):
                ref[...] = total[i * part : (i + 1) * part]

    def place(j, bit):
        return (1 - j + bit[0] * (2 * j - 1), 0)

    def fixed(j, bit):
        return (0, 0)

    return pl.pallas_call(
        kernel,
        grid_spec=pltpu.PrefetchScalarGridSpec(
            num_scalar_prefetch=1,
            grid=(2,),
            in_specs=[pl.BlockSpec((half, width), place)] * count,
            out_specs=[pl.BlockSpec((part, width), fixed)] * 4 + [pl.BlockSpec((half, 1), place)],
        ),
        out_shape=[jax.ShapeDtypeStruct((part, width), F32)] * 2
        + [jax.ShapeDtypeStruct((part, width), BF16)] * 2
        + [jax.ShapeDtypeStruct((rows, 1), F32)],
        compiler_params=pltpu.CompilerParams(**PARAMS),
        cost_estimate=LIGHT,
        name="unit_sums",
    )(bit, *in_hbm(grads))


def cotangent(bit, scale, n_member, kept, sent, got, turned_action, q, target, g):
    rows, width = g.shape
    half = rows // 2
    part = half // 2

    def kernel(bit_ref, *refs):
        kept_refs, sent_refs, got_refs, turned_action_ref = refs[:2], refs[2:4], refs[4:6], refs[6]
        q_ref, target_ref, g_ref, cot_ref, left_ref, resid_ref, length_ref, total_ref = refs[7:]
        resid_ref[...] = jnp.sum(q_ref[...], axis=-1, keepdims=True) - target_ref[...]
        step = pl.program_id(0)

        @pl.when(step == 0)
        def _():
            for i in range(2):
                total_ref[pl.ds(i * part, part), :] = kept_refs[i][...]
            left_ref[:, pl.ds(0, rows)] = turned_action_ref[...]

        @pl.when(step == 1)
        def _():
            for i in range(2):
                total_ref[pl.ds(i * part, part), :] = (
                    n_member * sent_refs[i][...].astype(F32) + got_refs[i][...].astype(F32)
                )

        total = total_ref[...]
        grad = g_ref[...]
        inverse = inverse_norm(grad)
        unit = grad * inverse
        direction = scale * (total - unit.astype(BF16).astype(F32))
        along = jnp.sum(unit * direction, axis=-1, keepdims=True)
        cot = (direction - unit * along) * inverse
        cot_ref[...] = cot.astype(BF16)
        turned = cot.T.astype(BF16)
        for place in range(2):

            @pl.when((step + bit_ref[0]) % 2 == place)
            def _():
                left_ref[:, pl.ds(rows + place * half, half)] = turned

        length_ref[...] = jnp.sum(total * total, axis=-1, keepdims=True)

    def place(j, bit):
        return (j + bit[0] * (1 - 2 * j), 0)

    def fixed(j, bit):
        return (0, 0)

    return pl.pallas_call(
        kernel,
        grid_spec=pltpu.PrefetchScalarGridSpec(
            num_scalar_prefetch=1,
            grid=(2,),
            in_specs=[pl.BlockSpec((part, width), fixed)] * 6
            + [
                pl.BlockSpec((width, rows), fixed),
                pl.BlockSpec((half, 128), place),
                pl.BlockSpec((half, 1), place),
                pl.BlockSpec((half, width), place),
            ],
            out_specs=[
                pl.BlockSpec((half, width), place),
                pl.BlockSpec((width, 2 * rows), fixed),
                pl.BlockSpec((half, 1), place),
                pl.BlockSpec((half, 1), place),
            ],
            scratch_shapes=[pltpu.VMEM((half, width), F32)],
        ),
        out_shape=[
            pltpu.HBM((rows, width), BF16),
            pltpu.HBM((width, 2 * rows), BF16),
            pltpu.HBM((rows, 1), F32),
            jax.ShapeDtypeStruct((rows, 1), F32),
        ],
        compiler_params=pltpu.CompilerParams(**PARAMS),
        cost_estimate=LIGHT,
        name="cotangent",
    )(bit, *kept, *sent, *got, *in_hbm([turned_action, q, target, g]))


def back(member, lo, cols, offset, cot, left, weight_a, pieces, value_w, pre, resid, grads, shape):
    rows, width = cot.shape
    size = pieces[0].shape[0]
    tile = min(TILE, cols)
    steps = cols // tile
    base, inner = lo // tile, offset // tile
    held = weight_a.shape[0]
    n_in = 6 + len(pieces)
    mid = width // 2
    part = min(256, tile)

    def kernel(*refs):
        cot_ref, left_ref, own_ref, value_ref, pre_ref, resid_ref = refs[:6]
        rest = refs[6:n_in]
        state_ref, sums_ref, top_ref, bottom_ref = refs[-5:-1]
        back_ref = refs[-1]
        starts = range(0, tile, part)
        for c in starts:
            lanes = pl.ds(c, part)
            weights = jnp.concatenate([own_ref[0, :, lanes]] + [r[:, lanes] for r in rest], axis=0)
            back_ref[:, lanes] = jnp.dot(cot_ref[...], weights, preferred_element_type=F32)
        for c in starts:
            lanes = pl.ds(c, part)
            value = value_ref[pl.ds(member, 1), lanes].astype(F32)
            sums = jnp.zeros((8, part), F32)
            dpres, tangents = [], []
            for r in range(0, rows, STRIP):
                cut = pl.ds(r, STRIP)
                hidden, one, two = slopes(pre_ref[cut, lanes])
                back_term = back_ref[cut, lanes]
                resid_here = resid_ref[cut, :]
                dpre = (value * (one * resid_here + two * back_term)).astype(BF16)
                state_ref[0, cut, lanes] = dpre
                term = hidden * resid_here + one * back_term
                for s in range(0, STRIP, 8):
                    sums = sums + term[s : s + 8]
                dpres.append(dpre)
                tangents.append((one * value).astype(BF16))
            sums_ref[0, :, lanes] = jnp.sum(sums, axis=0, keepdims=True)
            right = jnp.concatenate(dpres + tangents, axis=0)
            bottom_ref[:, lanes] = jnp.dot(
                left_ref[pl.ds(mid, mid), :], right, preferred_element_type=F32
            ).astype(BF16)
            top_ref[:, lanes] = jnp.dot(
                left_ref[pl.ds(0, mid), :], right, preferred_element_type=F32
            ).astype(BF16)

    piece = pl.BlockSpec((size, tile), lambda j: (0, inner + j))
    in_specs = [
        full((rows, width)),
        full((width, 2 * rows)),
        pl.BlockSpec((1, size, tile), lambda j: (member, 0, base + j)),
        pl.BlockSpec((held, tile), lambda j: (0, base + j)),
        pl.BlockSpec((rows, tile), lambda j: (0, inner + j)),
        full((rows, 1)),
    ] + [piece] * len(pieces)
    args = [cot, left, weight_a, value_w, pre, resid] + list(pieces)
    aliases = {}
    if grads is not None:
        in_specs += [pl.BlockSpec(memory_space=pl.ANY)] * 2
        args += list(grads)
        aliases = {n_in: 0, n_in + 1: 1}
    return pl.pallas_call(
        kernel,
        grid=(steps,),
        in_specs=in_specs,
        out_specs=[
            pl.BlockSpec((1, rows, tile), lambda j: (member, 0, base + j)),
            pl.BlockSpec((1, 1, tile), lambda j: (member, 0, base + j)),
            pl.BlockSpec((mid, tile), lambda j: (0, j)),
            pl.BlockSpec((mid, tile), lambda j: (0, j)),
        ],
        out_shape=[
            pltpu.HBM(shape, BF16),
            pltpu.HBM((held, 1, shape[-1]), F32),
            pltpu.HBM((mid, cols), BF16),
            jax.ShapeDtypeStruct((mid, cols), BF16),
        ],
        scratch_shapes=[pltpu.VMEM((rows, tile), F32)],
        input_output_aliases=aliases,
        compiler_params=pltpu.CompilerParams(**PARAMS),
        cost_estimate=LIGHT,
        name="back",
    )(*in_hbm(args[:6]), *args[6:])


def combine(size, jobs, final, weight_grad, shape):
    in_specs, args = [], []
    out_specs, out_shape = [], []

    def take(addends):
        cols = addends[0][0].shape[1]
        for i, (array, block) in enumerate(addends):
            array = array if i else in_hbm([array])[0]
            in_specs.append(pl.BlockSpec((size, cols), functools.partial(lambda b, *_: (b, 0), block)))
            args.append(array)
        return len(addends)

    counts = [[take(addends) for addends in job] for job in jobs]
    for job in jobs:
        cols = job[0][0][0].shape[1]
        out_specs.append(full((len(job) * size, cols)))
        out_shape.append(jax.ShapeDtypeStruct((len(job) * size, cols), BF16))
    if final is not None:
        member, lo, addends = final
        cols = addends[0][0].shape[1]
        counts.append([take(addends)])
        out_specs.append(pl.BlockSpec((1, size, cols), lambda *_: (member, 0, lo // cols)))
        out_shape.append(pltpu.HBM(shape, BF16))
    n_in = len(args)
    aliases = {}
    if final is not None and weight_grad is not None:
        in_specs.append(pl.BlockSpec(memory_space=pl.ANY))
        args.append(weight_grad)
        aliases = {n_in: len(jobs)}

    def kernel(*refs):
        outs = refs[len(args) :]
        at = 0
        for i, parts in enumerate(counts):
            for p, count in enumerate(parts):
                addends = refs[at : at + count]
                at += count
                for r in range(0, size, STRIP):
                    total = addends[0][pl.ds(r, STRIP), :].astype(F32)
                    for ref in addends[1:]:
                        total = total + ref[pl.ds(r, STRIP), :].astype(F32)
                    if i < len(jobs):
                        outs[i][pl.ds(p * size + r, STRIP), :] = total.astype(BF16)
                    else:
                        outs[i][0, pl.ds(r, STRIP), :] = total.astype(BF16)

    outs = pl.pallas_call(
        kernel,
        grid=(1,),
        in_specs=in_specs,
        out_specs=out_specs,
        out_shape=out_shape,
        input_output_aliases=aliases,
        compiler_params=pltpu.CompilerParams(**PARAMS),
        cost_estimate=LIGHT,
        name="combine",
    )(*args)
    return outs[: len(jobs)], (outs[-1] if final is not None else weight_grad)


def butterfly(x, axis, size, start=1):
    bit = start
    while bit < size:
        x = x + lax.ppermute(x, axis, [(i, i ^ bit) for i in range(size)])
        bit *= 2
    return x


def member_total(kept, sent, size):
    pair = [(i, i ^ 1) for i in range(size)]
    firsts = [lax.ppermute(x, "member", pair).astype(F32) for x in sent]
    totals = [a + b for a, b in zip(kept, firsts)]
    bit = 2
    while bit < size:
        swap = [(i, i ^ bit) for i in range(size)]
        totals = [x + lax.ppermute(x.astype(BF16), "member", swap).astype(F32) for x in totals]
        bit *= 2
    got = [lax.ppermute((x - size * first).astype(BF16), "member", pair) for x, first in zip(totals, firsts)]
    return totals, got


def body(n_member, n_row, action, state_term, target, weight_a, value_w):
    ring = Ring(n_row)
    chips, half = ring.chips, ring.half
    held, size, hidden_width = weight_a.shape
    members = held * n_member
    pairs = members * (members - 1)
    rows = action.shape[0]
    member_index = lax.axis_index("member")
    bit = (member_index % 2).astype(jnp.int32).reshape(1)
    action_here, turned_action = permute_action(action, ring.blocks())

    chunks = plan(GATHER_CUTS, held, hidden_width)
    count = len(chunks)
    pieces, pres, carry = {}, {}, [None] * held
    links, chains, swaps = [], {}, {}

    def send(x, *earlier):
        links.append(ring.onward(tie(x, *links[-2:-1], *earlier)))
        return links[-1]

    def run_front(c):
        m, lo, _ = chunks[c]
        pres[m, lo], *carry[m] = front(m, lo, action_here, state_term, weight_a, pieces[m, lo], value_w, carry[m])
        return carry[m][0]

    def open_chunk(c, *earlier):
        m, lo, cols = chunks[c]
        own = weight_a[m, :, lo : lo + cols]
        first = ring.partner(own)
        mine, a, b = [], own, first
        for _ in range(1, half):
            a = send(a, *earlier)
            b = send(b)
            mine += [a, b]
        chains[c] = (a, mine, first)
        swaps[c] = [ring.partner(x) for x in mine]

    def close_chunk(c):
        m, lo, _ = chunks[c]
        a, mine, first = chains[c]
        last = send(a)
        pieces[m, lo] = mine + [last, first] + swaps[c] + [ring.partner(last)]

    open_chunk(0)
    for c in range(1, count):
        open_chunk(c, *([run_front(c - 3)] if c >= 3 else []))
        close_chunk(c - 1)
    close_chunk(count - 1)
    for c in range(max(count - 3, 0), count):
        run_front(c)
    gs = [c[1] for c in carry]

    *kept_sent, square = unit_sums(bit, gs)
    kept, sent = kept_sent[:2], kept_sent[2:]
    totals, got = member_total(kept, sent, n_member)
    cots = [
        cotangent(bit, 2.0 * ETA / pairs, n_member, totals, sent, got, turned_action, q, target[:, None], g)
        for q, g in carry
    ]
    counted = ((jnp.arange(rows) // (rows // 2)) == bit[0]) & (member_index < 2)
    lengths = jnp.where(counted, cots[0][3][:, 0], 0.0) - square[:, 0]
    diversity = butterfly(lengths, "member", n_member) / pairs

    chunks = plan(SCATTER_CUTS, held, hidden_width)
    count = len(chunks)
    grads = weight_grad = None
    tops, others, flows, swapped = {}, {}, {}, {}
    queue = []

    def run_back(c, *earlier):
        nonlocal grads
        m, lo, cols = chunks[c]
        start = max(l for mm, l in pieces if mm == m and l <= lo)
        pre = tie(pres[m, start], *earlier) if earlier else pres[m, start]
        cot, left, resid, _ = cots[m]
        *grads, tops[c], bottom = back(
            m, lo, cols, lo - start, cot, left, weight_a, pieces[m, start],
            value_w, pre, resid, grads, state_term.shape,
        )
        others[c] = ring.partner(bottom)
        return bottom

    def addends(c, place, *more):
        return [(tops[c], place), (others[c], place), *more]

    lead = 2
    for c in range(lead):
        run_back(c)
    finish_at = {}
    for c in range(count):
        finish_at.setdefault(min(c + half + 1, count - 1 + half), []).append(c)
    after = None
    for s in range(count + half):
        jobs, labels = [], []
        for t in range(half):
            c = s - t
            if not 0 <= c < count:
                continue
            job = [addends(c, 2 * (half - t) - 1, *([(flows[c], 0)] if t else []))]
            if t:
                job.append(addends(c, 2 * (half - t), *([(flows[c], 1)] if t > 1 else [])))
            jobs.append(job)
            labels.append((c, t))
        if after is not None and jobs:
            tops[s] = tie(tops[s], after)
            jobs[0] = [addends(s, 2 * half - 1)]
        finals = [
            (chunks[c][0], chunks[c][1], addends(c, 0, (flows[c], 0), (swapped[c], 1)))
            for c in finish_at.get(s, [])
        ]
        for final in finals[:-1]:
            _, weight_grad = combine(size, [], final, weight_grad, weight_a.shape)
        outs, weight_grad = combine(size, jobs, finals[-1] if finals else None, weight_grad, weight_a.shape)
        after = None
        if s + lead < count:
            after = run_back(s + lead, outs[0])
        for (c, t), x in zip(labels, outs):
            flows[c] = ring.backward(tie(x, *queue[-2:-1]))
            queue.append(flows[c])
            if t == half - 1:
                swapped[c] = ring.partner(flows[c])
    value_grad = butterfly(grads[1][:, 0, :], "row", n_row)
    state_grad = grads[0]
    return weight_grad, value_grad, state_grad, diversity


def solution(mesh):
    in_specs = (
        P("row", None),
        P("member", "row", None),
        P("row"),
        P("member", "row", None),
        P("member", None),
    )
    out_specs = (P("member", "row", None), P("member", None), P("member", "row", None), P("row"))
    step = functools.partial(body, mesh.shape["member"], mesh.shape["row"])
    return jax.shard_map(step, mesh=mesh, in_specs=in_specs, out_specs=out_specs, check_vma=False)
```

time: 393 us -> 302 us (0.77)
  waiting for transfers between devices: 271 us -> 124 us
  Pallas kernels: 0 us -> 101 us
  matrix products: 64.7 us -> 0 us
  starting transfers between devices: 0.38 us -> 55.2 us
  blocking collectives: 24.6 us -> 0 us
  between operations: 14 us -> 1.26 us
  local copies, waits for them, and re-layouts: 5.6 us -> 17.2 us
  other arithmetic: 12.3 us -> 3.05 us
    all_gather x3 -> x0, waiting for transfers between devices: 181 us -> none  [the longest x2 100 us: body(): gathered = lax.all_gather(weight_a[member_pos], 'row', axis=0, tiled=True)]
    ppermute x0 -> x74, waiting for transfers between devices: none -> 124 us  [the longest x14 64.2 us: backward(): return lax.ppermute(x, 'row', self.down)]
    pallas_call x0 -> x26, Pallas kernels: none -> 101 us  [the longest x7 40 us: back(): pl.pallas_call(kernel, grid=(steps,), in_specs=in_specs, out_specs=[pl.Bl...]
    reduce_scatter x2 -> x0, waiting for transfers between devices: 89.7 us -> none  [body(): lax.psum_scatter(weight_term(left, right).astype(jnp.bfloat16), 'row', sc...]
    dot_general x9 -> x0, matrix products: 64.7 us -> none  [the longest x2 19.5 us: forward_member(): jnp.dot(action, weights, preferred_element_type=jnp.float32)]
    ppermute x0 -> x74, starting transfers between devices: none -> 55.2 us  [the longest x15 24 us: onward(): return lax.ppermute(x, 'row', self.up)]
    psum x1 -> x0, blocking collectives: 24.6 us -> none  [body(): lax.psum(jnp.stack(value_grads, axis=0).astype(jnp.bfloat16), 'row')]
    unnamed x24 -> x99, local copies, waits for them, and re-layouts: 2.45 us -> 13.5 us
  transfers between devices with their start and end apart: 5 -> 74, of which waited for: 5 -> 33; matrix products, arithmetic and copies ran while one was open for 11% -> 2% of each run, Pallas kernels for 0% -> 28%
where the time goes in v1:
time: 302 us; the launch traced here: 301 us
  waiting for transfers between devices  124 us (41%)
  Pallas kernels  101 us (33%)
  starting transfers between devices  55.2 us (18%)
  local copies, waits for them, and re-layouts  17.2 us (6%)
  other arithmetic  3.05 us (1%)
    ppermute x14, waiting for transfers between devices, backward(): return lax.ppermute(x, 'row', self.down)  64.2 us
    pallas_call x7, Pallas kernels, back(): pl.pallas_call(kernel, grid=(steps,), in_specs=in_specs, out_specs=[pl.Bl...  40 us
    ppermute x15, waiting for transfers between devices, onward(): return lax.ppermute(x, 'row', self.up)  38.2 us
    pallas_call x5, Pallas kernels, front(): pl.pallas_call(kernel, grid=(steps,), in_specs=in_specs, out_specs=[pl.Bl...  30.3 us
    ppermute x15, starting transfers between devices, onward(): return lax.ppermute(x, 'row', self.up)  24 us
    pallas_call x10, Pallas kernels, combine(): pl.pallas_call(kernel, grid=(1,), in_specs=in_specs, out_specs=out_specs,...  18.7 us
    unnamed x99, local copies, waits for them, and re-layouts  13.5 us
    ppermute x14, starting transfers between devices, backward(): return lax.ppermute(x, 'row', self.down)  12.3 us
  transfers between devices with their start and end apart: 74, of which 33 were waited for; matrix products, arithmetic and copies ran while one was open for 2% of the time, Pallas kernels for 28%

profile of v1, /device:TPU:0, one launch (start us, length us, event | category | flops | bytes accessed | tf_op | source)
XLA Modules:
  0.0 301.2 jit_solution(5692509132163210009)
XLA Ops:
  7.1 5.3 %collective-permute-done.refs_4_.refs_6_ = bf16[128,2048]{1,0:T(8,128)(2,1)S(1)} collective-permute-done((bf16[128,2048]{1,0:T(8,128)(2,1)S(1)}, bf16[128,2048]{1,0:T(8,128)(2,1)S(1)}, u32[]{:S(2)}, u32[]{:S(2)}) %collective-permute-start) | collective-permute-done | bytes 524320 | tf_op jit(solution)/shard_map/ppermute | solution.py:59
  14.4 3.6 %collective-permute-done.4.refs_5_.refs_7_ = bf16[128,2048]{1,0:T(8,128)(2,1)S(1)} collective-permute-done((bf16[128,2048]{1,0:T(8,128)(2,1)S(1)}, bf16[128,2048]{1,0:T(8,128)(2,1)S(1)}, u32[]{:S(2)}, u32[]{:S(2)}) %collective-permute-start.4) | collective-permute-done | bytes 524320 | tf_op jit(solution)/shard_map/ppermute | solution.py:59
  25.8 3.5 %collective-permute-done.5.refs_5_.refs_7_ = bf16[128,2048]{1,0:T(8,128)(2,1)S(1)} collective-permute-done((bf16[128,2048]{1,0:T(8,128)(2,1)S(1)}, bf16[128,2048]{1,0:T(8,128)(2,1)S(1)}, u32[]{:S(2)}, u32[]{:S(2)}) %collective-permute-start.5) | collective-permute-done | bytes 524320 | tf_op jit(solution)/shard_map/ppermute | solution.py:59
  37.0 3.7 %collective-permute-done.6.refs_4_.refs_6_ = bf16[128,2048]{1,0:T(8,128)(2,1)} collective-permute-done((bf16[128,2048]{1,0:T(8,128)(2,1)S(1)}, bf16[128,2048]{1,0:T(8,128)(2,1)}, u32[]{:S(2)}, u32[]{:S(2)}) %collective-permute-start.6) | collective-permute-done | bytes 524320 | tf_op jit(solution)/shard_map/ppermute | solution.py:59
  47.5 6.5 %front.5 = (f32[256,2048]{1,0:T(8,128)}, f32[256,128]{1,0:T(8,128)}, f32[256,1024]{1,0:T(8,128)}) custom-call(bf16[256,1024]{1,0:T(8,128)(2,1)} %copy-done, bf16[2,256,4096]{2,1,0:T(8,128)(2,1)} %refs_1_.9, bf16[2,128,4096]{2,1,0:T(8,128)(2,1)} %refs_2_.23, bf16[2,4096]{1,0:T(2,128)(2,1)} %refs_3_.23, ...), custom_call_target="tpu_custom_call" | custom-call | flops 1000000 | bytes 100000 | tf_op jit(solution)/shard_map/front/pallas_call | solution.py:195
  56.6 3.8 %collective-permute-done.21.refs_4_.refs_6_ = bf16[128,1024]{1,0:T(8,128)(2,1)S(1)} collective-permute-done((bf16[128,1024]{1,0:T(8,128)(2,1)S(1)}, bf16[128,1024]{1,0:T(8,128)(2,1)S(1)}, u32[]{:S(2)}, u32[]{:S(2)}) %collective-permute-start.21) | collective-permute-done | bytes 262176 | tf_op jit(solution)/shard_map/ppermute | solution.py:59
  62.6 7.3 %front.6 = (f32[256,2048]{1,0:T(8,128)}, f32[256,128]{1,0:T(8,128)}, f32[256,1024]{1,0:T(8,128)}) custom-call(bf16[256,1024]{1,0:T(8,128)(2,1)} %copy-done, bf16[2,256,4096]{2,1,0:T(8,128)(2,1)} %refs_1_.9, bf16[2,128,4096]{2,1,0:T(8,128)(2,1)} %refs_2_.23, bf16[2,4096]{1,0:T(2,128)(2,1)} %refs_3_.23, ...), custom_call_target="tpu_custom_call", output_to_operand_aliasing={{1}: (11, {}), {2}: (12, {})} | custom-call | flops 1000000 | bytes 100000 | tf_op jit(solution)/shard_map/front/pallas_call | solution.py:195
  75.4 3.8 %collective-permute-done.17.refs_4_.refs_6_ = bf16[128,1024]{1,0:T(8,128)(2,1)} collective-permute-done((bf16[128,1024]{1,0:T(8,128)(2,1)S(1)}, bf16[128,1024]{1,0:T(8,128)(2,1)}, u32[]{:S(2)}, u32[]{:S(2)}) %collective-permute-start.17) | collective-permute-done | bytes 262176 | tf_op jit(solution)/shard_map/ppermute | solution.py:59
  95.5 6.7 %front.7 = (f32[256,2048]{1,0:T(8,128)}, f32[256,128]{1,0:T(8,128)}, f32[256,1024]{1,0:T(8,128)}) custom-call(bf16[256,1024]{1,0:T(8,128)(2,1)} %copy-done, bf16[2,256,4096]{2,1,0:T(8,128)(2,1)} %refs_1_.9, bf16[2,128,4096]{2,1,0:T(8,128)(2,1)} %refs_2_.23, bf16[2,4096]{1,0:T(2,128)(2,1)} %refs_3_.23, ...), custom_call_target="tpu_custom_call" | custom-call | flops 1000000 | bytes 100000 | tf_op jit(solution)/shard_map/front/pallas_call | solution.py:195
  102.2 4.9 %front.8 = (f32[256,1024]{1,0:T(8,128)}, f32[256,128]{1,0:T(8,128)}, f32[256,1024]{1,0:T(8,128)}) custom-call(bf16[256,1024]{1,0:T(8,128)(2,1)} %copy-done, bf16[2,256,4096]{2,1,0:T(8,128)(2,1)} %refs_1_.9, bf16[2,128,4096]{2,1,0:T(8,128)(2,1)} %refs_2_.23, bf16[2,4096]{1,0:T(2,128)(2,1)} %refs_3_.23, ...), custom_call_target="tpu_custom_call", output_to_operand_aliasing={{1}: (11, {}), {2}: (12, {})} | custom-call | flops 1000000 | bytes 100000 | tf_op jit(solution)/shard_map/front/pallas_call | solution.py:195
  107.1 4.9 %front.9 = (f32[256,1024]{1,0:T(8,128)}, f32[256,128]{1,0:T(8,128)}, f32[256,1024]{1,0:T(8,128)}) custom-call(bf16[256,1024]{1,0:T(8,128)(2,1)} %copy-done, bf16[2,256,4096]{2,1,0:T(8,128)(2,1)} %refs_1_.9, bf16[2,128,4096]{2,1,0:T(8,128)(2,1)} %refs_2_.23, bf16[2,4096]{1,0:T(2,128)(2,1)} %refs_3_.23, ...), custom_call_target="tpu_custom_call", output_to_operand_aliasing={{1}: (11, {}), {2}: (12, {})} | custom-call | flops 1000000 | bytes 100000 | tf_op jit(solution)/shard_map/front/pallas_call | solution.py:195
  117.0 4.3 %collective-permute-done.35 = bf16[64,1024]{1,0:T(8,128)(2,1)S(1)} collective-permute-done((bf16[64,1024]{1,0:T(8,128)(2,1)S(1)}, bf16[64,1024]{1,0:T(8,128)(2,1)S(1)}, u32[]{:S(2)}, u32[]{:S(2)}) %collective-permute-start.35) | collective-permute-done | bytes 131104 | tf_op jit(solution)/shard_map/ppermute | solution.py:498
  126.7 7.1 %collective-permute-done.36 = bf16[64,1024]{1,0:T(8,128)(2,1)S(1)} collective-permute-done((bf16[64,1024]{1,0:T(8,128)(2,1)S(1)}, bf16[64,1024]{1,0:T(8,128)(2,1)S(1)}, u32[]{:S(2)}, u32[]{:S(2)}) %collective-permute-start.36) | collective-permute-done | bytes 131104 | tf_op jit(solution)/shard_map/ppermute | solution.py:503
  144.1 3.9 %cotangent.3 = (bf16[256,1024]{1,0:T(8,128)(2,1)}, bf16[1024,512]{1,0:T(8,128)(2,1)}, f32[256,1]{1,0:T(8,128)}, f32[256,1]{1,0:T(8,128)S(1)}) custom-call(s32[1]{0:T(128)} %bitcast.bit_ref, f32[64,1024]{1,0:T(8,128)S(1)} %get-tuple-element.227.refs_0_, f32[64,1024]{1,0:T(8,128)S(1)} %copy-done.1, bf16[64,1024]{1,0:T(8,128)(2,1)S(1)} %get-tuple-element.138.refs_2_, ...), custom_call_target="tpu_custom_call" | custom-call | flops 1000000 | bytes 100000 | tf_op jit(solution)/shard_map/cotangent/pallas_call | solution.py:310
  148.0 3.8 %back.7 = (bf16[2,256,4096]{2,1,0:T(8,128)(2,1)}, f32[2,1,4096]{2,1,0:T(1,128)}, bf16[512,512]{1,0:T(8,128)(2,1)}, bf16[512,512]{1,0:T(8,128)(2,1)S(1)}) custom-call(bf16[256,1024]{1,0:T(8,128)(2,1)} %get-tuple-element.147.refs_0_, bf16[1024,512]{1,0:T(8,128)(2,1)} %get-tuple-element.148.refs_1_, bf16[2,128,4096]{2,1,0:T(8,128)(2,1)} %refs_2_.23, ...), custom_call_target="tpu_custom_call" | custom-call | flops 1000000 | bytes 100000 | tf_op jit(solution)/shard_map/back/pallas_call | solution.py:404
  151.8 3.7 %back.8 = (bf16[2,256,4096]{2,1,0:T(8,128)(2,1)}, f32[2,1,4096]{2,1,0:T(1,128)}, bf16[512,512]{1,0:T(8,128)(2,1)}, bf16[512,512]{1,0:T(8,128)(2,1)S(1)}) custom-call(bf16[256,1024]{1,0:T(8,128)(2,1)} %get-tuple-element.147.refs_0_, bf16[1024,512]{1,0:T(8,128)(2,1)} %get-tuple-element.148.refs_1_, ...), custom_call_target="tpu_custom_call", output_to_operand_aliasing={{0}: (13, {}), {1}: (14, {})} | custom-call | flops 1000000 | bytes 100000 | tf_op jit(solution)/shard_map/back/pallas_call | solution.py:404
  157.0 5.2 %back.9 = (bf16[2,256,4096]{2,1,0:T(8,128)(2,1)}, f32[2,1,4096]{2,1,0:T(1,128)}, bf16[512,1024]{1,0:T(8,128)(2,1)}, bf16[512,1024]{1,0:T(8,128)(2,1)S(1)}) custom-call(bf16[256,1024]{1,0:T(8,128)(2,1)} %get-tuple-element.147.refs_0_, bf16[1024,512]{1,0:T(8,128)(2,1)} %get-tuple-element.148.refs_1_, ...), custom_call_target="tpu_custom_call", output_to_operand_aliasing={{0}: (13, {}), {1}: (14, {})} | custom-call | flops 1000000 | bytes 100000 | tf_op jit(solution)/shard_map/back/pallas_call | solution.py:404
  162.9 4.4 %collective-permute-done.43.refs_4_ = bf16[128,512]{1,0:T(8,128)(2,1)S(1)} collective-permute-done((bf16[128,512]{1,0:T(8,128)(2,1)S(1)}, bf16[128,512]{1,0:T(8,128)(2,1)S(1)}, u32[]{:S(2)}, u32[]{:S(2)}) %collective-permute-start.43) | collective-permute-done | bytes 131104 | tf_op jit(solution)/shard_map/ppermute | solution.py:62
  168.5 8.3 %back.10 = (bf16[2,256,4096]{2,1,0:T(8,128)(2,1)}, f32[2,1,4096]{2,1,0:T(1,128)}, bf16[512,2048]{1,0:T(8,128)(2,1)}, bf16[512,2048]{1,0:T(8,128)(2,1)S(1)}) custom-call(bf16[256,1024]{1,0:T(8,128)(2,1)} %get-tuple-element.147.refs_0_, bf16[1024,512]{1,0:T(8,128)(2,1)} %get-tuple-element.148.refs_1_, ...), custom_call_target="tpu_custom_call", output_to_operand_aliasing={{0}: (13, {}), {1}: (14, {})} | custom-call | flops 1000000 | bytes 100000 | tf_op jit(solution)/shard_map/back/pallas_call | solution.py:404
  177.6 3.9 %cotangent.2 = (bf16[256,1024]{1,0:T(8,128)(2,1)}, bf16[1024,512]{1,0:T(8,128)(2,1)}, f32[256,1]{1,0:T(8,128)}, f32[256,1]{1,0:T(8,128)}) custom-call(s32[1]{0:T(128)} %bitcast.bit_ref, f32[64,1024]{1,0:T(8,128)S(1)} %get-tuple-element.227.refs_0_, f32[64,1024]{1,0:T(8,128)S(1)} %copy-done.2, bf16[64,1024]{1,0:T(8,128)(2,1)S(1)} %get-tuple-element.138.refs_2_, ...), custom_call_target="tpu_custom_call" | custom-call | flops 1000000 | bytes 100000 | tf_op jit(solution)/shard_map/cotangent/pallas_call | solution.py:310
  183.4 8.2 %back.11 = (bf16[2,256,4096]{2,1,0:T(8,128)(2,1)}, f32[2,1,4096]{2,1,0:T(1,128)}, bf16[512,2048]{1,0:T(8,128)(2,1)}, bf16[512,2048]{1,0:T(8,128)(2,1)S(1)}) custom-call(bf16[256,1024]{1,0:T(8,128)(2,1)} %get-tuple-element.143.refs_0_, bf16[1024,512]{1,0:T(8,128)(2,1)} %get-tuple-element.144.refs_1_, ...), custom_call_target="tpu_custom_call", output_to_operand_aliasing={{0}: (13, {}), {1}: (14, {})} | custom-call | flops 1000000 | bytes 100000 | tf_op jit(solution)/shard_map/back/pallas_call | solution.py:404
  193.1 5.7 %collective-permute-done.48.refs_9_ = bf16[256,512]{1,0:T(8,128)(2,1)S(1)} collective-permute-done((bf16[256,512]{1,0:T(8,128)(2,1)S(1)}, bf16[256,512]{1,0:T(8,128)(2,1)S(1)}, u32[]{:S(2)}, u32[]{:S(2)}) %collective-permute-start.48) | collective-permute-done | bytes 262176 | tf_op jit(solution)/shard_map/ppermute | solution.py:62
  201.0 4.2 %collective-permute-done.47.refs_4_ = bf16[128,1024]{1,0:T(8,128)(2,1)S(1)} collective-permute-done((bf16[128,1024]{1,0:T(8,128)(2,1)S(1)}, bf16[128,1024]{1,0:T(8,128)(2,1)S(1)}, u32[]{:S(2)}, u32[]{:S(2)}) %collective-permute-start.47) | collective-permute-done | bytes 262176 | tf_op jit(solution)/shard_map/ppermute | solution.py:62
  209.3 5.4 %back.12 = (bf16[2,256,4096]{2,1,0:T(8,128)(2,1)}, f32[2,1,4096]{2,1,0:T(1,128)}, bf16[512,1024]{1,0:T(8,128)(2,1)}, bf16[512,1024]{1,0:T(8,128)(2,1)S(1)}) custom-call(bf16[256,1024]{1,0:T(8,128)(2,1)} %get-tuple-element.143.refs_0_, bf16[1024,512]{1,0:T(8,128)(2,1)} %get-tuple-element.144.refs_1_, ...), custom_call_target="tpu_custom_call", output_to_operand_aliasing={{0}: (13, {}), {1}: (14, {})} | custom-call | flops 1000000 | bytes 100000 | tf_op jit(solution)/shard_map/back/pallas_call | solution.py:404
  218.7 3.2 %collective-permute-done.57.refs_9_ = bf16[256,1024]{1,0:T(8,128)(2,1)S(1)} collective-permute-done((bf16[256,1024]{1,0:T(8,128)(2,1)S(1)}, bf16[256,1024]{1,0:T(8,128)(2,1)S(1)}, u32[]{:S(2)}, u32[]{:S(2)}) %collective-permute-start.57) | collective-permute-done | bytes 524320 | tf_op jit(solution)/shard_map/ppermute | solution.py:62
  224.1 5.4 %back.13 = (bf16[2,256,4096]{2,1,0:T(8,128)(2,1)}, f32[2,1,4096]{2,1,0:T(1,128)}, bf16[512,1024]{1,0:T(8,128)(2,1)}, bf16[512,1024]{1,0:T(8,128)(2,1)S(1)}) custom-call(bf16[256,1024]{1,0:T(8,128)(2,1)} %get-tuple-element.143.refs_0_, bf16[1024,512]{1,0:T(8,128)(2,1)} %get-tuple-element.144.refs_1_, ...), custom_call_target="tpu_custom_call", output_to_operand_aliasing={{0}: (13, {}), {1}: (14, {})} | custom-call | flops 1000000 | bytes 100000 | tf_op jit(solution)/shard_map/back/pallas_call | solution.py:404
  229.5 12.8 %collective-permute-done.56.refs_4_ = bf16[128,2048]{1,0:T(8,128)(2,1)S(1)} collective-permute-done((bf16[128,2048]{1,0:T(8,128)(2,1)S(1)}, bf16[128,2048]{1,0:T(8,128)(2,1)S(1)}, u32[]{:S(2)}, u32[]{:S(2)}) %collective-permute-start.56) | collective-permute-done | bytes 524320 | tf_op jit(solution)/shard_map/ppermute | solution.py:62
  245.9 13.6 %collective-permute-done.63.refs_7_ = bf16[256,2048]{1,0:T(8,128)(2,1)S(1)} collective-permute-done((bf16[256,2048]{1,0:T(8,128)(2,1)S(1)}, bf16[256,2048]{1,0:T(8,128)(2,1)S(1)}, u32[]{:S(2)}, u32[]{:S(2)}) %collective-permute-start.63) | collective-permute-done | bytes 1048608 | tf_op jit(solution)/shard_map/ppermute | solution.py:62
  260.2 5.7 %collective-permute-done.59.refs_4_ = bf16[128,1024]{1,0:T(8,128)(2,1)S(1)} collective-permute-done((bf16[128,1024]{1,0:T(8,128)(2,1)S(1)}, bf16[128,1024]{1,0:T(8,128)(2,1)S(1)}, u32[]{:S(2)}, u32[]{:S(2)}) %collective-permute-start.59) | collective-permute-done | bytes 262176 | tf_op jit(solution)/shard_map/ppermute | solution.py:62
  270.6 4.2 %collective-permute-done.62.refs_2_ = bf16[128,1024]{1,0:T(8,128)(2,1)S(1)} collective-permute-done((bf16[128,1024]{1,0:T(8,128)(2,1)S(1)}, bf16[128,1024]{1,0:T(8,128)(2,1)S(1)}, u32[]{:S(2)}, u32[]{:S(2)}) %collective-permute-start.62) | collective-permute-done | bytes 262176 | tf_op jit(solution)/shard_map/ppermute | solution.py:62
  280.4 6.2 %collective-permute-done.65.refs_2_ = bf16[256,1024]{1,0:T(8,128)(2,1)S(1)} collective-permute-done((bf16[256,1024]{1,0:T(8,128)(2,1)}, bf16[256,1024]{1,0:T(8,128)(2,1)S(1)}, u32[]{:S(2)}, u32[]{:S(2)}) %collective-permute-start.65) | collective-permute-done | bytes 524320 | tf_op jit(solution)/shard_map/ppermute | solution.py:62
  287.9 3.2 %collective-permute-done.72 = f32[256]{0:T(256)S(1)} collective-permute-done((f32[256]{0:T(256)S(1)}, f32[256]{0:T(256)S(1)}, u32[]{:S(2)}, u32[]{:S(2)}) %collective-permute-start.72) | collective-permute-done | bytes 1056 | tf_op jit(solution)/shard_map/ppermute | solution.py:491
  (257 shorter events, 123.3 us)
Async XLA Ops:
  5.4 12.6 %collective-permute-start.4 = (bf16[128,2048]{1,0:T(8,128)(2,1)S(1)}, bf16[128,2048]{1,0:T(8,128)(2,1)S(1)}, u32[]{:S(2)}, u32[]{:S(2)}) collective-permute-start(bf16[128,2048]{1,0:T(8,128)(2,1)S(1)} %collective-permute-done.3.refs_7_.refs_9_), channel_id=1, source_target_pairs={{0,2},{1,5},{2,6},{3,1},{6,4},{7,3},{4,0},{5,7},{8,10},{9,13},{10,... | collective-permute-start | bytes 1572872 | tf_op jit(solution)/shard_map/ppermute | solution.py:59
  12.4 11.3 %collective-permute-start.1 = (bf16[128,2048]{1,0:T(8,128)(2,1)S(1)}, bf16[128,2048]{1,0:T(8,128)(2,1)}, u32[]{:S(2)}, u32[]{:S(2)}) collective-permute-start(bf16[128,2048]{1,0:T(8,128)(2,1)S(1)} %get-tuple-element.115), channel_id=1, source_target_pairs={{0,2},{1,5},{2,6},{3,1},{6,4},{7,3},{4,0},{5,7},{8,10},{9,13},{10,... | collective-permute-start | bytes 1572872 | tf_op jit(solution)/shard_map/ppermute | solution.py:59
  29.3 11.3 %collective-permute-start.6 = (bf16[128,2048]{1,0:T(8,128)(2,1)S(1)}, bf16[128,2048]{1,0:T(8,128)(2,1)}, u32[]{:S(2)}, u32[]{:S(2)}) collective-permute-start(bf16[128,2048]{1,0:T(8,128)(2,1)S(1)} %get-tuple-element.117), channel_id=1, source_target_pairs={{0,2},{1,5},{2,6},{3,1},{6,4},{7,3},{4,0},{5,7},{8,10},{9,13},{10,... | collective-permute-start | bytes 1572872 | tf_op jit(solution)/shard_map/ppermute | solution.py:59
  31.3 16.2 %collective-permute-start.12 = (bf16[128,2048]{1,0:T(8,128)(2,1)S(1)}, bf16[128,2048]{1,0:T(8,128)(2,1)S(1)}, u32[]{:S(2)}, u32[]{:S(2)}) collective-permute-start(bf16[128,2048]{1,0:T(8,128)(2,1)S(1)} %collective-permute-done.refs_4_.refs_6_), channel_id=1, source_target_pairs={{0,1},{1,0},{2,3},{3,2},{6,7},{7,6},{4,5},{5,4},{8,9},{9,8},{10,11... | collective-permute-start | bytes 1572872 | tf_op jit(solution)/shard_map/ppermute | solution.py:65
  31.3 16.2 %collective-permute-start.13 = (bf16[128,2048]{1,0:T(8,128)(2,1)S(1)}, bf16[128,2048]{1,0:T(8,128)(2,1)S(1)}, u32[]{:S(2)}, u32[]{:S(2)}) collective-permute-start(bf16[128,2048]{1,0:T(8,128)(2,1)S(1)} %collective-permute-done.4.refs_5_.refs_7_), channel_id=1, source_target_pairs={{0,1},{1,0},{2,3},{3,2},{6,7},{7,6},{4,5},{5,4},{8,9},{9,8},{10,11... | collective-permute-start | bytes 1572872 | tf_op jit(solution)/shard_map/ppermute | solution.py:65
  34.9 12.6 %collective-permute-start.14 = (bf16[128,2048]{1,0:T(8,128)(2,1)S(1)}, bf16[128,2048]{1,0:T(8,128)(2,1)}, u32[]{:S(2)}, u32[]{:S(2)}) collective-permute-start(bf16[128,2048]{1,0:T(8,128)(2,1)S(1)} %collective-permute-done.11.refs_6_.refs_8_), channel_id=1, source_target_pairs={{0,1},{1,0},{2,3},{3,2},{6,7},{7,6},{4,5},{5,4},{8,9},{9,8},{10,11... | collective-permute-start | bytes 1572872 | tf_op jit(solution)/shard_map/ppermute | solution.py:65
  34.9 19.1 %collective-permute-start.20 = (bf16[128,2048]{1,0:T(8,128)(2,1)}, bf16[128,2048]{1,0:T(8,128)(2,1)}, u32[]{:S(2)}, u32[]{:S(2)}) collective-permute-start(bf16[128,2048]{1,0:T(8,128)(2,1)} %collective-permute-done.19.refs_7_.refs_9_), channel_id=1, source_target_pairs={{0,2},{1,5},{2,6},{3,1},{6,4},{7,3},{4,0},{5,7},{8,10},{9,13},{10,... | collective-permute-start | bytes 1572872 | tf_op jit(solution)/shard_map/ppermute | solution.py:59
  40.6 15.5 %collective-permute-start.7 = (bf16[128,2048]{1,0:T(8,128)(2,1)}, bf16[128,2048]{1,0:T(8,128)(2,1)}, u32[]{:S(2)}, u32[]{:S(2)}) collective-permute-start(bf16[128,2048]{1,0:T(8,128)(2,1)} %collective-permute-done.1.refs_4_.refs_6_), channel_id=1, source_target_pairs={{0,2},{1,5},{2,6},{3,1},{6,4},{7,3},{4,0},{5,7},{8,10},{9,13},{10,... | collective-permute-start | bytes 1572872 | tf_op jit(solution)/shard_map/ppermute | solution.py:59
  60.4 13.8 %collective-permute-start.22 = (bf16[128,2048]{1,0:T(8,128)(2,1)}, bf16[128,2048]{1,0:T(8,128)(2,1)S(1)}, u32[]{:S(2)}, u32[]{:S(2)}) collective-permute-start(bf16[128,2048]{1,0:T(8,128)(2,1)} %collective-permute-done.6.refs_4_.refs_6_), channel_id=1, source_target_pairs={{0,2},{1,5},{2,6},{3,1},{6,4},{7,3},{4,0},{5,7},{8,10},{9,13},{10,... | collective-permute-start | bytes 1572872 | tf_op jit(solution)/shard_map/ppermute | solution.py:59
  62.5 11.8 %collective-permute-start.18 = (bf16[128,1024]{1,0:T(8,128)(2,1)S(1)}, bf16[128,1024]{1,0:T(8,128)(2,1)S(1)}, u32[]{:S(2)}, u32[]{:S(2)}) collective-permute-start(bf16[128,1024]{1,0:T(8,128)(2,1)S(1)} %get-tuple-element.125), channel_id=1, source_target_pairs={{0,1},{1,0},{2,3},{3,2},{6,7},{7,6},{4,5},{5,4},{8,9},{9,8},{10,11... | collective-permute-start | bytes 786440 | tf_op jit(solution)/shard_map/ppermute | solution.py:65
  74.9 13.6 %collective-permute-start.32 = (bf16[128,2048]{1,0:T(8,128)(2,1)}, bf16[128,2048]{1,0:T(8,128)(2,1)S(1)}, u32[]{:S(2)}, u32[]{:S(2)}) collective-permute-start(bf16[128,2048]{1,0:T(8,128)(2,1)} %collective-permute-done.6.refs_4_.refs_6_), channel_id=1, source_target_pairs={{0,1},{1,0},{2,3},{3,2},{6,7},{7,6},{4,5},{5,4},{8,9},{9,8},{10,11... | collective-permute-start | bytes 1572872 | tf_op jit(solution)/shard_map/ppermute | solution.py:65
  85.6 16.5 %collective-permute-start.30 = (bf16[128,1024]{1,0:T(8,128)(2,1)}, bf16[128,1024]{1,0:T(8,128)(2,1)}, u32[]{:S(2)}, u32[]{:S(2)}) collective-permute-start(bf16[128,1024]{1,0:T(8,128)(2,1)} %collective-permute-done.16.refs_5_.refs_7_), channel_id=1, source_target_pairs={{0,1},{1,0},{2,3},{3,2},{6,7},{7,6},{4,5},{5,4},{8,9},{9,8},{10,11... | collective-permute-start | bytes 786440 | tf_op jit(solution)/shard_map/ppermute | solution.py:65
  88.5 13.7 %collective-permute-start.31 = (bf16[128,1024]{1,0:T(8,128)(2,1)}, bf16[128,1024]{1,0:T(8,128)(2,1)}, u32[]{:S(2)}, u32[]{:S(2)}) collective-permute-start(bf16[128,1024]{1,0:T(8,128)(2,1)} %collective-permute-done.28.refs_6_.refs_8_), channel_id=1, source_target_pairs={{0,1},{1,0},{2,3},{3,2},{6,7},{7,6},{4,5},{5,4},{8,9},{9,8},{10,11... | collective-permute-start | bytes 786440 | tf_op jit(solution)/shard_map/ppermute | solution.py:65
  89.4 17.8 %collective-permute-start.26 = (bf16[128,1024]{1,0:T(8,128)(2,1)}, bf16[128,1024]{1,0:T(8,128)(2,1)}, u32[]{:S(2)}, u32[]{:S(2)}) collective-permute-start(bf16[128,1024]{1,0:T(8,128)(2,1)} %collective-permute-done.23.refs_5_.refs_7_), channel_id=1, source_target_pairs={{0,1},{1,0},{2,3},{3,2},{6,7},{7,6},{4,5},{5,4},{8,9},{9,8},{10,11... | collective-permute-start | bytes 786440 | tf_op jit(solution)/shard_map/ppermute | solution.py:65
  90.7 16.4 %collective-permute-start.25 = (bf16[128,1024]{1,0:T(8,128)(2,1)}, bf16[128,1024]{1,0:T(8,128)(2,1)}, u32[]{:S(2)}, u32[]{:S(2)}) collective-permute-start(bf16[128,1024]{1,0:T(8,128)(2,1)} %collective-permute-done.17.refs_4_.refs_6_), channel_id=1, source_target_pairs={{0,1},{1,0},{2,3},{3,2},{6,7},{7,6},{4,5},{5,4},{8,9},{9,8},{10,11... | collective-permute-start | bytes 786440 | tf_op jit(solution)/shard_map/ppermute | solution.py:65
  91.3 15.8 %collective-permute-start.27 = (bf16[128,1024]{1,0:T(8,128)(2,1)}, bf16[128,1024]{1,0:T(8,128)(2,1)}, u32[]{:S(2)}, u32[]{:S(2)}) collective-permute-start(bf16[128,1024]{1,0:T(8,128)(2,1)} %collective-permute-done.24.refs_6_.refs_8_), channel_id=1, source_target_pairs={{0,1},{1,0},{2,3},{3,2},{6,7},{7,6},{4,5},{5,4},{8,9},{9,8},{10,11... | collective-permute-start | bytes 786440 | tf_op jit(solution)/shard_map/ppermute | solution.py:65
  121.3 12.5 %collective-permute-start.36 = (bf16[64,1024]{1,0:T(8,128)(2,1)S(1)}, bf16[64,1024]{1,0:T(8,128)(2,1)S(1)}, u32[]{:S(2)}, u32[]{:S(2)}) collective-permute-start(bf16[64,1024]{1,0:T(8,128)(2,1)S(1)} %fusion.4), channel_id=1, source_target_pairs={{0,16},{8,24},{16,0},{24,8},{1,17},{9,25},{17,1},{25,9},{2,18},{10... | collective-permute-start | bytes 393224 | tf_op jit(solution)/shard_map/ppermute | solution.py:503
  123.9 11.5 %collective-permute-start.38 = (bf16[64,1024]{1,0:T(8,128)(2,1)S(1)}, bf16[64,1024]{1,0:T(8,128)(2,1)S(1)}, u32[]{:S(2)}, u32[]{:S(2)}) collective-permute-start(bf16[64,1024]{1,0:T(8,128)(2,1)S(1)} %fusion.5), channel_id=1, source_target_pairs={{0,16},{8,24},{16,0},{24,8},{1,17},{9,25},{17,1},{25,9},{2,18},{10... | collective-permute-start | bytes 393224 | tf_op jit(solution)/shard_map/ppermute | solution.py:503
  162.2 19.9 %collective-permute-start.44 = (bf16[512,1024]{1,0:T(8,128)(2,1)S(1)}, bf16[512,1024]{1,0:T(8,128)(2,1)S(1)}, u32[]{:S(2)}, u32[]{:S(2)}) collective-permute-start(bf16[512,1024]{1,0:T(8,128)(2,1)S(1)} %get-tuple-element.161), channel_id=1, source_target_pairs={{0,1},{1,0},{2,3},{3,2},{6,7},{7,6},{4,5},{5,4},{8,9},{9,8},{10,11... | collective-permute-start | bytes 3145736 | tf_op jit(solution)/shard_map/ppermute | solution.py:65
  176.8 28.4 %collective-permute-start.46 = (bf16[512,2048]{1,0:T(8,128)(2,1)S(1)}, bf16[512,2048]{1,0:T(8,128)(2,1)S(1)}, u32[]{:S(2)}, u32[]{:S(2)}) collective-permute-start(bf16[512,2048]{1,0:T(8,128)(2,1)S(1)} %get-tuple-element.168), channel_id=1, source_target_pairs={{0,1},{1,0},{2,3},{3,2},{6,7},{7,6},{4,5},{5,4},{8,9},{9,8},{10,11... | collective-permute-start | bytes 6291464 | tf_op jit(solution)/shard_map/ppermute | solution.py:65
  191.7 24.7 %collective-permute-start.50 = (bf16[512,2048]{1,0:T(8,128)(2,1)S(1)}, bf16[512,2048]{1,0:T(8,128)(2,1)S(1)}, u32[]{:S(2)}, u32[]{:S(2)}) collective-permute-start(bf16[512,2048]{1,0:T(8,128)(2,1)S(1)} %get-tuple-element.178), channel_id=1, source_target_pairs={{0,1},{1,0},{2,3},{3,2},{6,7},{7,6},{4,5},{5,4},{8,9},{9,8},{10,11... | collective-permute-start | bytes 6291464 | tf_op jit(solution)/shard_map/ppermute | solution.py:65
  208.0 13.9 %collective-permute-start.57 = (bf16[256,1024]{1,0:T(8,128)(2,1)S(1)}, bf16[256,1024]{1,0:T(8,128)(2,1)S(1)}, u32[]{:S(2)}, u32[]{:S(2)}) collective-permute-start(bf16[256,1024]{1,0:T(8,128)(2,1)S(1)} %get-tuple-element.203), channel_id=1, source_target_pairs={{0,4},{1,3},{2,0},{3,7},{6,2},{7,5},{4,6},{5,1},{8,12},{9,11},{10,... | collective-permute-start | bytes 1572872 | tf_op jit(solution)/shard_map/ppermute | solution.py:62
  214.7 14.8 %collective-permute-start.55 = (bf16[512,1024]{1,0:T(8,128)(2,1)S(1)}, bf16[512,1024]{1,0:T(8,128)(2,1)S(1)}, u32[]{:S(2)}, u32[]{:S(2)}) collective-permute-start(bf16[512,1024]{1,0:T(8,128)(2,1)S(1)} %get-tuple-element.187), channel_id=1, source_target_pairs={{0,1},{1,0},{2,3},{3,2},{6,7},{7,6},{4,5},{5,4},{8,9},{9,8},{10,11... | collective-permute-start | bytes 3145736 | tf_op jit(solution)/shard_map/ppermute | solution.py:65
  221.9 22.8 %collective-permute-start.60 = (bf16[256,2048]{1,0:T(8,128)(2,1)S(1)}, bf16[256,2048]{1,0:T(8,128)(2,1)S(1)}, u32[]{:S(2)}, u32[]{:S(2)}) collective-permute-start(bf16[256,2048]{1,0:T(8,128)(2,1)S(1)} %get-tuple-element.208), channel_id=1, source_target_pairs={{0,4},{1,3},{2,0},{3,7},{6,2},{7,5},{4,6},{5,1},{8,12},{9,11},{10,... | collective-permute-start | bytes 3145736 | tf_op jit(solution)/shard_map/ppermute | solution.py:62
  222.6 19.8 %collective-permute-start.56 = (bf16[128,2048]{1,0:T(8,128)(2,1)S(1)}, bf16[128,2048]{1,0:T(8,128)(2,1)S(1)}, u32[]{:S(2)}, u32[]{:S(2)}) collective-permute-start(bf16[128,2048]{1,0:T(8,128)(2,1)S(1)} %get-tuple-element.201), channel_id=1, source_target_pairs={{0,4},{1,3},{2,0},{3,7},{6,2},{7,5},{4,6},{5,1},{8,12},{9,11},{10,... | collective-permute-start | bytes 1572872 | tf_op jit(solution)/shard_map/ppermute | solution.py:62
  244.8 14.8 %collective-permute-start.63 = (bf16[256,2048]{1,0:T(8,128)(2,1)S(1)}, bf16[256,2048]{1,0:T(8,128)(2,1)S(1)}, u32[]{:S(2)}, u32[]{:S(2)}) collective-permute-start(bf16[256,2048]{1,0:T(8,128)(2,1)S(1)} %get-tuple-element.213), channel_id=1, source_target_pairs={{0,4},{1,3},{2,0},{3,7},{6,2},{7,5},{4,6},{5,1},{8,12},{9,11},{10,... | collective-permute-start | bytes 3145736 | tf_op jit(solution)/shard_map/ppermute | solution.py:62
  245.4 20.5 %collective-permute-start.54 = (bf16[512,1024]{1,0:T(8,128)(2,1)S(1)}, bf16[512,1024]{1,0:T(8,128)(2,1)S(1)}, u32[]{:S(2)}, u32[]{:S(2)}) collective-permute-start(bf16[512,1024]{1,0:T(8,128)(2,1)S(1)} %get-tuple-element.198), channel_id=1, source_target_pairs={{0,1},{1,0},{2,3},{3,2},{6,7},{7,6},{4,5},{5,4},{8,9},{9,8},{10,11... | collective-permute-start | bytes 3145736 | tf_op jit(solution)/shard_map/ppermute | solution.py:65
  245.4 20.5 %collective-permute-start.61 = (bf16[256,2048]{1,0:T(8,128)(2,1)S(1)}, bf16[256,2048]{1,0:T(8,128)(2,1)S(1)}, u32[]{:S(2)}, u32[]{:S(2)}) collective-permute-start(bf16[256,2048]{1,0:T(8,128)(2,1)S(1)} %collective-permute-done.60.refs_9_), channel_id=1, source_target_pairs={{0,1},{1,0},{2,3},{3,2},{6,7},{7,6},{4,5},{5,4},{8,9},{9,8},{10,11... | collective-permute-start | bytes 3145736 | tf_op jit(solution)/shard_map/ppermute | solution.py:65
  259.6 15.2 %collective-permute-start.64 = (bf16[256,2048]{1,0:T(8,128)(2,1)S(1)}, bf16[256,2048]{1,0:T(8,128)(2,1)S(1)}, u32[]{:S(2)}, u32[]{:S(2)}) collective-permute-start(bf16[256,2048]{1,0:T(8,128)(2,1)S(1)} %collective-permute-done.63.refs_7_), channel_id=1, source_target_pairs={{0,1},{1,0},{2,3},{3,2},{6,7},{7,6},{4,5},{5,4},{8,9},{9,8},{10,11... | collective-permute-start | bytes 3145736 | tf_op jit(solution)/shard_map/ppermute | solution.py:65
  269.1 11.3 %collective-permute-start.67 = (bf16[256,1024]{1,0:T(8,128)(2,1)}, bf16[256,1024]{1,0:T(8,128)(2,1)S(1)}, u32[]{:S(2)}, u32[]{:S(2)}) collective-permute-start(bf16[256,1024]{1,0:T(8,128)(2,1)} %get-tuple-element.218), channel_id=1, source_target_pairs={{0,4},{1,3},{2,0},{3,7},{6,2},{7,5},{4,6},{5,1},{8,12},{9,11},{10,... | collective-permute-start | bytes 1572872 | tf_op jit(solution)/shard_map/ppermute | solution.py:62
  280.4 17.3 %collective-permute-start.68 = (bf16[256,1024]{1,0:T(8,128)(2,1)S(1)}, bf16[256,1024]{1,0:T(8,128)(2,1)S(1)}, u32[]{:S(2)}, u32[]{:S(2)}) collective-permute-start(bf16[256,1024]{1,0:T(8,128)(2,1)S(1)} %collective-permute-done.67.refs_2_), channel_id=1, source_target_pairs={{0,1},{1,0},{2,3},{3,2},{6,7},{7,6},{4,5},{5,4},{8,9},{9,8},{10,11... | collective-permute-start | bytes 1572872 | tf_op jit(solution)/shard_map/ppermute | solution.py:65
  286.7 12.8 %collective-permute-start.66 = (bf16[256,1024]{1,0:T(8,128)(2,1)S(1)}, bf16[256,1024]{1,0:T(8,128)(2,1)S(1)}, u32[]{:S(2)}, u32[]{:S(2)}) collective-permute-start(bf16[256,1024]{1,0:T(8,128)(2,1)S(1)} %collective-permute-done.65.refs_2_), channel_id=1, source_target_pairs={{0,1},{1,0},{2,3},{3,2},{6,7},{7,6},{4,5},{5,4},{8,9},{9,8},{10,11... | collective-permute-start | bytes 1572872 | tf_op jit(solution)/shard_map/ppermute | solution.py:65
  (91 other events, 580.3 us)

commit v2 on v0

v2 whole, which is shorter than its diff:
```python
import functools

import jax
import jax.numpy as jnp
from jax import lax
from jax.experimental import pallas as pl
from jax.experimental.pallas import tpu as pltpu
from jax.sharding import PartitionSpec as P

EPS = 1e-06
ETA = 5.0
UNIT = 512
GATHER_CUTS = ((2, 2, 2, 2), (2, 2, 2, 1, 1))
SCATTER_CUTS = ((1, 1, 2, 2, 2), (2, 2, 2, 1, 1))
LANES = 512
STRIP = 16
F32 = jnp.float32
BF16 = jnp.bfloat16
FLOPS_PER_US = 1153500000


def tie(x, *earlier):
    return lax.optimization_barrier((x,) + earlier)[0]


def in_vmem(xs):
    return [pltpu.with_memory_space_constraint(x, pltpu.VMEM) for x in xs]


def resident(kernel, name, ins, outs, scalars=(), scratch=(), hbm=(), aliases=None, micros=0.7):
    spaces = [pltpu.SMEM] * len(scalars) + [pltpu.VMEM] * len(ins) + [pl.ANY] * len(hbm)
    return pl.pallas_call(
        kernel,
        in_specs=[pl.BlockSpec(memory_space=space) for space in spaces],
        out_specs=[pl.BlockSpec(memory_space=pl.ANY if x.hbm else pltpu.VMEM) for x in outs],
        out_shape=[(pltpu.HBM if x.hbm else pltpu.VMEM)(x.shape, x.dtype) for x in outs],
        scratch_shapes=list(scratch),
        input_output_aliases=aliases or {},
        compiler_params=pltpu.CompilerParams(vmem_limit_bytes=5 * 1024 * 1024),
        cost_estimate=pl.CostEstimate(flops=int(micros * FLOPS_PER_US), bytes_accessed=0, transcendentals=0),
        name=name,
    )(*scalars, *in_vmem(ins), *hbm)


class Out:
    def __init__(self, shape, dtype, hbm=False):
        self.shape, self.dtype, self.hbm = shape, dtype, hbm


def plan(cuts, held, width):
    out = []
    for m in range(held):
        lo = 0
        for units in cuts[0] if m < held - 1 else cuts[1]:
            out.append((m, lo, units * UNIT))
            lo += units * UNIT
        assert lo == width
    return out


class Ring:
    def __init__(self, n_row):
        self.n_row = n_row
        self.chips = n_row // 2
        self.half = self.chips // 2
        order = list(range(self.half)) + [self.chips + self.half - 1 - p for p in range(self.half, self.chips)]
        up, down, swap = [], [], []
        for pos in range(self.chips):
            for core in range(2):
                here = order[pos] * 2 + core
                step = 1 - 2 * core
                up.append((here, order[(pos + step) % self.chips] * 2 + core))
                down.append((here, order[(pos - step) % self.chips] * 2 + core))
                swap.append((here, order[pos] * 2 + 1 - core))
        self.up, self.down, self.swap = up, down, swap

    def onward(self, x):
        return lax.ppermute(x, "row", self.up)

    def backward(self, x):
        return lax.ppermute(x, "row", self.down)

    def partner(self, x):
        return lax.ppermute(x, "row", self.swap)

    def blocks(self, me):
        chip, core = lax.div(me, 2), lax.rem(me, 2)
        flip = self.chips + self.half - 1
        pos = jnp.where(chip < self.half, chip, flip - chip)

        def index(p, c):
            p = lax.rem(p + 2 * self.chips, self.chips)
            return jnp.where(p < self.half, p, flip - p) * 2 + c

        out = []
        for c, step in ((core, 1 - 2 * core), (1 - core, 2 * core - 1)):
            out.append(index(pos, c))
            for t in range(1, self.half):
                out.append(index(pos - step * t, c))
                out.append(index(pos - step * t, 1 - c))
            out.append(index(pos - step * self.half, c))
        return out


def slopes(pre):
    turn = jnp.tanh(0.5 * pre)
    sig = 0.5 * turn + 0.5
    rest = 1.0 - sig
    spread = sig * rest
    one = sig + pre * spread
    two = spread * (2.0 - pre * turn)
    return pre * sig, one, two


def inverse_norm(g):
    return 1.0 / jnp.sqrt(jnp.sum(g * g, axis=-1, keepdims=True) + EPS)


def strips(start, rows):
    return [pl.ds(start + r, STRIP) for r in range(0, rows, STRIP)]


def spans(cols):
    step = LANES if cols > LANES else cols // 2
    return [pl.ds(c, step) for c in range(0, cols, step)]


def cut_out(weight_a, places, info, *earlier):
    size = weight_a.shape[1]

    def kernel(*refs):
        weight_ref, sems = refs[1], refs[-1]
        copies = []
        for i, (m, lo, cols) in enumerate(places):
            out_ref = refs[2 + len(earlier) + i]
            copies.append(pltpu.make_async_copy(weight_ref.at[m, :, pl.ds(lo, cols)], out_ref, sems.at[i]))
            copies[-1].start()
        for copy in copies:
            copy.wait()

    return resident(
        kernel,
        "cut_out",
        [],
        [Out((size, cols), BF16) for _, _, cols in places],
        [info],
        [pltpu.SemaphoreType.DMA((len(places),))],
        [weight_a, *earlier],
    )


def permute_action(action, ring, info):
    rows, width = action.shape
    count = 2 * ring.chips
    size = width // count
    if size % 128:
        order = jnp.stack(ring.blocks(info[0]))
        moved = jnp.take(action.reshape(rows, count, size), order, axis=1).reshape(rows, width)
        return moved, moved.T

    def kernel(info_ref, x_ref, out_ref, turned_ref):
        for j, block in enumerate(ring.blocks(info_ref[0])):
            x = x_ref[:, pl.ds(pl.multiple_of(block * size, size), size)]
            out_ref[:, pl.ds(j * size, size)] = x
            turned_ref[pl.ds(j * size, size), :] = x.astype(F32).T.astype(BF16)

    return resident(
        kernel, "permute_action", [action], [Out((rows, width), BF16), Out((width, rows), BF16)], [info]
    )


def front(member, lo, action, state, pieces, value_w, carry):
    rows, width = action.shape
    size, cols = pieces[0].shape
    n_in = 3 + len(pieces)

    def kernel(*refs):
        action_ref, state_ref, value_ref = refs[:3]
        rest = refs[3:n_in]
        q_ref, g_ref, pre_ref, tangent_ref = refs[-4:]

        def weights(span):
            return jnp.concatenate([r[:, span] for r in rest], axis=0)

        for span in spans(cols):
            pre_ref[:, span] = jnp.dot(action_ref[...], weights(span), preferred_element_type=F32)
        for i, span in enumerate(spans(cols)):
            here = pl.ds(lo + span.start, span.size)
            value = value_ref[pl.ds(member, 1), here].astype(F32)
            for cut in strips(0, rows):
                pre = pre_ref[cut, span] + state_ref[member, cut, here].astype(F32)
                hidden, one, _ = slopes(pre)
                prod = hidden * value
                lanes = prod[:, :128]
                for c in range(128, span.size, 128):
                    lanes = lanes + prod[:, c : c + 128]
                if i:
                    lanes = lanes + q_ref[cut, :]
                elif carry is not None:
                    lanes = lanes + refs[n_in][cut, :]
                q_ref[cut, :] = lanes
                tangent_ref[cut, span] = (one * value).astype(BF16)
            g = lax.dot_general(
                tangent_ref[:, span], weights(span), (((1,), (1,)), ((), ())), preferred_element_type=F32
            )
            if i:
                g = g + g_ref[...]
            elif carry is not None:
                g = g + refs[n_in + 1][...]
            g_ref[...] = g

    ins = [action, state, value_w, *pieces, *(carry or [])]
    return resident(
        kernel,
        "front",
        ins,
        [Out((rows, 128), F32), Out((rows, width), F32)],
        scratch=[pltpu.VMEM((rows, cols), F32), pltpu.VMEM((rows, cols), BF16)],
        aliases={} if carry is None else {n_in: 0, n_in + 1: 1},
        micros=cols / 512,
    )


def unit_sums(info, grads):
    rows, width = grads[0].shape
    half = rows // 2
    part = half // 2

    def kernel(info_ref, *refs):
        bit = lax.rem(info_ref[1], 2)
        g_refs, outs, square_ref = refs[:-5], refs[-5:-1], refs[-1]
        for i, out_ref in enumerate(outs):
            side = bit if i < 2 else 1 - bit
            for r in range(0, part, STRIP):
                cut = pl.ds(pl.multiple_of(side * half + (i % 2) * part + r, STRIP), STRIP)
                total, square = None, None
                for g_ref in g_refs:
                    g = g_ref[cut, :]
                    unit = (g * inverse_norm(g)).astype(BF16).astype(F32)
                    length = jnp.sum(unit * unit, axis=-1, keepdims=True)
                    total = unit if total is None else total + unit
                    square = length if square is None else square + length
                square_ref[cut, :] = square
                out_ref[pl.ds(r, STRIP), :] = total.astype(out_ref.dtype)

    outs = [Out((part, width), F32)] * 2 + [Out((part, width), BF16)] * 2 + [Out((rows, 1), F32)]
    return resident(kernel, "unit_sums", grads, outs, [info])


def add_part(kept, got, scale, minus):
    def kernel(kept_ref, got_ref, *refs):
        total_ref, sent_ref = refs[-2:]
        for cut in strips(0, kept.shape[0]):
            total = kept_ref[cut, :] + got_ref[cut, :].astype(F32)
            total_ref[cut, :] = total
            if minus is not None:
                total = total - scale * refs[0][cut, :].astype(F32)
            sent_ref[cut, :] = total.astype(BF16)

    ins = [kept, got] + ([] if minus is None else [minus])
    return resident(kernel, "add_part", ins, [Out(kept.shape, F32), Out(kept.shape, BF16)])


def cotangent(info, members, n_member, kept, sent, got, turned_action, square, q, target, g):
    rows, width = g.shape
    half = rows // 2
    part = half // 2

    pairs = members * (members - 1)
    scale = 2.0 * ETA / pairs

    def kernel(info_ref, *refs):
        bit = lax.rem(info_ref[1], 2)
        counted = jnp.where(info_ref[1] < 2, 1.0, 0.0)
        kept_refs, sent_refs, got_refs, turned_action_ref = refs[:2], refs[2:4], refs[4:6], refs[6]
        square_ref, q_ref, target_ref, g_ref, cot_ref, left_ref, resid_ref, addend_ref, cot32_ref = refs[7:]
        resid_ref[...] = jnp.sum(q_ref[...], axis=-1, keepdims=True) - target_ref[...]
        left_ref[:, pl.ds(0, rows)] = turned_action_ref[...]
        for i in range(4):
            side = bit if i < 2 else 1 - bit
            for r in range(0, part, STRIP):
                here = pl.ds(r, STRIP)
                cut = pl.ds(pl.multiple_of(side * half + (i % 2) * part + r, STRIP), STRIP)
                if i < 2:
                    total = kept_refs[i][here, :]
                else:
                    total = n_member * sent_refs[i - 2][here, :].astype(F32) + got_refs[i - 2][here, :].astype(F32)
                grad = g_ref[cut, :]
                inverse = inverse_norm(grad)
                unit = grad * inverse
                direction = scale * (total - unit.astype(BF16).astype(F32))
                along = jnp.sum(unit * direction, axis=-1, keepdims=True)
                cot = (direction - unit * along) * inverse
                cot32_ref[cut, :] = cot
                cot_ref[cut, :] = cot.astype(BF16)
                addend = -square_ref[cut, :]
                if i < 2:
                    addend = addend + counted * jnp.sum(total * total, axis=-1, keepdims=True)
                addend_ref[cut, :] = addend * (1.0 / pairs)
        for r in range(0, rows, 128):
            left_ref[:, pl.ds(rows + r, 128)] = cot32_ref[pl.ds(r, 128), :].T.astype(BF16)

    return resident(
        kernel,
        "cotangent",
        [*kept, *sent, *got, turned_action, square, q, target, g],
        [Out((rows, width), BF16), Out((width, 2 * rows), BF16), Out((rows, 1), F32), Out((rows, 1), F32)],
        [info],
        [pltpu.VMEM((rows, width), F32)],
    )


def back(member, lo, cols, offset, action, state, cot, left, pieces, value_w, resid, grads):
    rows, width = cot.shape
    held = value_w.shape[0]
    n_in = 6 + len(pieces)
    mid = width // 2

    def kernel(*refs):
        action_ref, state_ref, cot_ref, left_ref, value_ref, resid_ref = refs[:6]
        rest = refs[6:n_in]
        grad_ref, sums_ref, top_ref, bottom_ref, pre_ref, back_ref, dpre_ref, tangent_ref, sems = refs[-9:]
        copies = []
        for span in spans(cols):
            inner = pl.ds(offset + span.start, span.size)
            weights = jnp.concatenate([r[:, inner] for r in rest], axis=0)
            pre_ref[:, span] = jnp.dot(action_ref[...], weights, preferred_element_type=F32)
            back_ref[:, span] = jnp.dot(cot_ref[...], weights, preferred_element_type=F32)
        for i, span in enumerate(spans(cols)):
            here = pl.ds(lo + span.start, span.size)
            value = value_ref[pl.ds(member, 1), here].astype(F32)
            sums = jnp.zeros((8, span.size), F32)
            for cut in strips(0, rows):
                hidden, one, two = slopes(pre_ref[cut, span] + state_ref[member, cut, here].astype(F32))
                back_term = back_ref[cut, span]
                resid_here = resid_ref[cut, :]
                dpre_ref[cut, span] = (value * (one * resid_here + two * back_term)).astype(BF16)
                tangent_ref[cut, span] = (one * value).astype(BF16)
                term = hidden * resid_here + one * back_term
                for s in range(0, STRIP, 8):
                    sums = sums + term[s : s + 8]
            sums_ref[member, :, here] = jnp.sum(sums, axis=0, keepdims=True)
            copies.append(pltpu.make_async_copy(dpre_ref.at[:, span], grad_ref.at[member, :, here], sems.at[i]))
            copies[-1].start()
            right = jnp.concatenate([dpre_ref[:, span], tangent_ref[:, span]], axis=0)
            bottom_ref[:, span] = jnp.dot(
                left_ref[pl.ds(mid, mid), :], right, preferred_element_type=F32
            ).astype(BF16)
            top_ref[:, span] = jnp.dot(left_ref[pl.ds(0, mid), :], right, preferred_element_type=F32).astype(BF16)
        for copy in copies:
            copy.wait()

    ins = [action, state, cot, left, value_w, resid, *pieces]
    hbm, aliases = [], {}
    if grads is not None:
        ins.append(grads[1])
        hbm.append(grads[0])
        aliases = {n_in: 1, n_in + 1: 0}
    return resident(
        kernel,
        "back",
        ins,
        [
            Out(state.shape, BF16, hbm=True),
            Out((held, 1, state.shape[-1]), F32),
            Out((mid, cols), BF16),
            Out((mid, cols), BF16),
        ],
        scratch=[
            pltpu.VMEM((rows, cols), F32),
            pltpu.VMEM((rows, cols), F32),
            pltpu.VMEM((rows, cols), BF16),
            pltpu.VMEM((rows, cols), BF16),
            pltpu.SemaphoreType.DMA((len(spans(cols)),)),
        ],
        hbm=hbm,
        aliases=aliases,
        micros=cols / 400,
    )


def combine(size, jobs, final, weight_grad, shape):
    ins, outs, scratch = [], [], []
    places = {}

    def take(addends):
        out = []
        for array, block in addends:
            if id(array) not in places:
                places[id(array)] = len(ins)
                ins.append(array)
            out.append((places[id(array)], block))
        return out

    sums = [[take(addends) for addends in job] for job in jobs]
    for job in jobs:
        outs.append(Out((len(job) * size, job[0][0][0].shape[1]), BF16))
    hbm, aliases = [], {}
    if final is not None:
        member, lo, addends = final
        cols = addends[0][0].shape[1]
        last = take(addends)
        outs.append(Out(shape, BF16, hbm=True))
        scratch = [pltpu.VMEM((size, cols), BF16), pltpu.SemaphoreType.DMA(())]
        if weight_grad is not None:
            hbm.append(weight_grad)
            aliases = {len(ins): len(jobs)}

    def kernel(*refs):
        results = refs[len(ins) + len(hbm) :]

        def add(addends, r):
            total = None
            for i, block in addends:
                x = refs[i][pl.ds(block * size + r, STRIP), :].astype(F32)
                total = x if total is None else total + x
            return total.astype(BF16)

        if final is not None:
            held_ref, sem = results[-2:]
            for r in range(0, size, STRIP):
                held_ref[pl.ds(r, STRIP), :] = add(last, r)
            copy = pltpu.make_async_copy(held_ref, results[len(jobs)].at[member, :, pl.ds(lo, cols)], sem)
            copy.start()
        for i, job in enumerate(sums):
            for p, addends in enumerate(job):
                for r in range(0, size, STRIP):
                    results[i][pl.ds(p * size + r, STRIP), :] = add(addends, r)
        if final is not None:
            copy.wait()

    got = resident(kernel, "combine", ins, outs, scratch=scratch, hbm=hbm, aliases=aliases)
    return got[: len(jobs)], (got[-1] if final is not None else weight_grad)


def exchange(x, axis, size, bit):
    def kernel(x_ref, y_ref, out_ref):
        out_ref[...] = x_ref[...] + y_ref[...]

    other = lax.ppermute(x, axis, [(i, i ^ bit) for i in range(size)])
    return resident(kernel, "add_two", [x, other], [Out(x.shape, x.dtype)])[0]


def member_total(kept, sent, size):
    pair = [(i, i ^ 1) for i in range(size)]
    firsts = [lax.ppermute(x, "member", pair) for x in sent]
    totals, got = list(kept), list(firsts)
    bit = 1
    while bit < size:
        bit *= 2
        swap = [(i, i ^ bit) for i in range(size)] if bit < size else pair
        for i in range(len(totals)):
            totals[i], x = add_part(totals[i], got[i], size, None if bit < size else firsts[i])
            got[i] = lax.ppermute(x, "member", swap)
    return totals, got


def body(n_member, n_row, action, state_term, target, weight_a, value_w):
    ring = Ring(n_row)
    chips, half = ring.chips, ring.half
    held, size, hidden_width = weight_a.shape
    members = held * n_member
    info = jnp.stack([lax.axis_index("row"), lax.axis_index("member")]).astype(jnp.int32)
    target_col = target[:, None]

    chunks = plan(GATHER_CUTS, held, hidden_width)
    count = len(chunks)
    owns = cut_out(weight_a, chunks[:1], info, target_col)
    owns += cut_out(weight_a, chunks[1:], info, owns[0])
    action_here, turned_action = permute_action(action, ring, info)
    pieces, carry = {}, [None] * held
    links, chains, swaps = [], {}, {}

    def send(x, *earlier):
        links.append(ring.onward(tie(x, *links[-3:-2], *earlier)))
        return links[-1]

    def run_front(c):
        m, lo, _ = chunks[c]
        carry[m] = front(m, lo, action_here, state_term, pieces[m, lo], value_w, carry[m])
        return carry[m][0]

    def open_chunk(c, *earlier):
        m, lo, cols = chunks[c]
        own = owns[c]
        first = ring.partner(own)
        mine, a, b = [], own, first
        for _ in range(1, half):
            a = send(a, *earlier)
            b = send(b)
            mine += [a, b]
        chains[c] = (a, mine, first)
        swaps[c] = [ring.partner(x) for x in mine]

    def close_chunk(c):
        m, lo, _ = chunks[c]
        a, mine, first = chains[c]
        last = send(a)
        pieces[m, lo] = [owns[c]] + mine + [last, first] + swaps[c] + [ring.partner(last)]

    open_chunk(0)
    for c in range(1, count):
        open_chunk(c, *([run_front(c - 3)] if c >= 3 else []))
        close_chunk(c - 1)
    close_chunk(count - 1)
    for c in range(max(count - 3, 0), count):
        run_front(c)
    gs = [c[1] for c in carry]

    *kept_sent, square = unit_sums(info, gs)
    kept, sent = kept_sent[:2], kept_sent[2:]
    totals, got = member_total(kept, sent, n_member)
    cots = [
        cotangent(info, members, n_member, totals, sent, got, turned_action, square, q, target_col, g)
        for q, g in carry
    ]
    diversity = cots[0][3]

    chunks = plan(SCATTER_CUTS, held, hidden_width)
    count = len(chunks)
    grads = weight_grad = None
    tops, others, flows, swapped = {}, {}, {}, {}
    queue = []

    def run_back(c, *earlier):
        nonlocal grads
        m, lo, cols = chunks[c]
        start = max(l for mm, l in pieces if mm == m and l <= lo)
        cot, left, resid, _ = cots[m]
        if earlier:
            resid = tie(resid, *earlier)
        *grads, tops[c], bottom = back(
            m, lo, cols, lo - start, action_here, state_term, cot, left, pieces[m, start],
            value_w, resid, grads,
        )
        others[c] = ring.partner(bottom)
        return bottom

    def addends(c, place, *more):
        return [(tops[c], place), (others[c], place), *more]

    lead = 3
    for c in range(lead - 1):
        run_back(c, *([x[0] for x in cots] if c else []))
    steps = count + 2 * half - 1
    finish_at = {}
    for c in range(count):
        finish_at.setdefault(min(c + 2 * half, steps - 1), []).append(c)
    after, value_grads = None, []
    stages, last_row = n_row.bit_length() - 1, count + 1 - lead
    for s in range(steps):
        jobs, labels = [], []
        if last_row <= s and len(value_grads) < stages + 1:
            value_grads.append(exchange(value_grads[-1], "row", n_row, 1 << (len(value_grads) - 1)))
            tops[s - 2] = tie(tops[s - 2], value_grads[-1])
        if s in (5, 6):
            diversity = exchange(diversity, "member", n_member, s - 4)
            tops[s] = tie(tops[s], diversity)
        if after is not None and s < count:
            tops[s] = tie(tops[s], after)
        for t in range(half):
            c = s - 2 * t
            if not 0 <= c < count:
                continue
            job = [addends(c, 2 * (half - t) - 1, *([(flows[c], 0)] if t else []))]
            if t:
                job.append(addends(c, 2 * (half - t), *([(flows[c], 1)] if t > 1 else [])))
            jobs.append(job)
            labels.append((c, t))
        finals = [
            (chunks[c][0], chunks[c][1], addends(c, 0, (flows[c], 0), (swapped[c], 1)))
            for c in finish_at.get(s, [])
        ]
        for final in finals[:-1]:
            _, weight_grad = combine(size, [], final, weight_grad, weight_a.shape)
        outs, weight_grad = combine(size, jobs, finals[-1] if finals else None, weight_grad, weight_a.shape)
        after = None
        if s == 0:
            run_back(lead - 1, outs[0])
        if s + lead < count:
            after = run_back(s + lead, outs[0])
            if s + lead == count - 1:
                value_grads = [grads[1]]
        for (c, t), x in zip(labels, outs):
            flows[c] = ring.backward(tie(x, *queue[-3:-2]))
            queue.append(flows[c])
            if t == half - 1:
                swapped[c] = ring.partner(flows[c])
    value_grad = value_grads[-1]
    while len(value_grads) < stages + 1:
        value_grad = exchange(value_grad, "row", n_row, 1 << (len(value_grads) - 1))
        value_grads.append(value_grad)
    bit = 4
    while bit < n_member:
        diversity = exchange(diversity, "member", n_member, bit)
        bit *= 2
    state_grad = grads[0]
    return weight_grad, value_grad[:, 0, :], state_grad, diversity[:, 0]


def solution(mesh):
    in_specs = (
        P("row", None),
        P("member", "row", None),
        P("row"),
        P("member", "row", None),
        P("member", None),
    )
    out_specs = (P("member", "row", None), P("member", None), P("member", "row", None), P("row"))
    step = functools.partial(body, mesh.shape["member"], mesh.shape["row"])
    return jax.shard_map(step, mesh=mesh, in_specs=in_specs, out_specs=out_specs, check_vma=False)
```

time: 393 us -> 272 us (0.69)
  waiting for transfers between devices: 271 us -> 121 us
  starting transfers between devices: 0.38 us -> 89.3 us
  matrix products: 64.7 us -> 0 us
  Pallas kernels: 0 us -> 53.6 us
  blocking collectives: 24.6 us -> 0 us
  between operations: 14 us -> 1.55 us
  other arithmetic: 12.3 us -> 0.76 us
    all_gather x3 -> x0, waiting for transfers between devices: 181 us -> none  [the longest x2 100 us: body(): gathered = lax.all_gather(weight_a[member_pos], 'row', axis=0, tiled=True)]
    ppermute x0 -> x114, waiting for transfers between devices: none -> 121 us  [the longest x20 48 us: backward(): return lax.ppermute(x, 'row', self.down)]
    reduce_scatter x2 -> x0, waiting for transfers between devices: 89.7 us -> none  [body(): lax.psum_scatter(weight_term(left, right).astype(jnp.bfloat16), 'row', sc...]
    ppermute x0 -> x114, starting transfers between devices: none -> 89.3 us  [the longest x27 49.3 us: onward(): return lax.ppermute(x, 'row', self.up)]
    dot_general x9 -> x0, matrix products: 64.7 us -> none  [the longest x2 19.5 us: forward_member(): jnp.dot(action, weights, preferred_element_type=jnp.float32)]
    pallas_call x0 -> x48, Pallas kernels: none -> 53.6 us  [resident(): pl.pallas_call(kernel, in_specs=[pl.BlockSpec(memory_space=space) for spa...]
    psum x1 -> x0, blocking collectives: 24.6 us -> none  [body(): lax.psum(jnp.stack(value_grads, axis=0).astype(jnp.bfloat16), 'row')]
    another operation x5 -> x1, other arithmetic: 6.83 us -> 0.08 us  [body(): jnp.stack([lax.axis_index('row'), lax.axis_index('member')])]
  transfers between devices with their start and end apart: 5 -> 114, of which waited for: 5 -> 46; matrix products, arithmetic and copies ran while one was open for 11% -> 0% of each run, Pallas kernels for 0% -> 16%
where the time goes in v2:
time: 272 us; the launch traced here: 269 us
  waiting for transfers between devices  121 us (44%)
  starting transfers between devices  89.3 us (33%)
  Pallas kernels  53.6 us (20%)
  local copies, waits for them, and re-layouts  3.05 us (1%)
    pallas_call x48, Pallas kernels, resident(): pl.pallas_call(kernel, in_specs=[pl.BlockSpec(memory_space=space) for spa...  53.6 us
    ppermute x27, starting transfers between devices, onward(): return lax.ppermute(x, 'row', self.up)  49.3 us
    ppermute x20, waiting for transfers between devices, backward(): return lax.ppermute(x, 'row', self.down)  48 us
    ppermute x27, waiting for transfers between devices, onward(): return lax.ppermute(x, 'row', self.up)  35.2 us
    ppermute x5, waiting for transfers between devices, exchange(): other = lax.ppermute(x, axis, [(i, i ^ bit) for i in range(size)])  19.7 us
    ppermute x20, starting transfers between devices, backward(): return lax.ppermute(x, 'row', self.down)  18.9 us
    ppermute x4, waiting for transfers between devices, member_total(): got[i] = lax.ppermute(x, 'member', swap)  13.7 us
    ppermute x56, starting transfers between devices, partner(): return lax.ppermute(x, 'row', self.swap)  8.32 us
  transfers between devices with their start and end apart: 114, of which 46 were waited for; matrix products, arithmetic and copies ran while one was open for 0% of the time, Pallas kernels for 16%

profile of v2, /device:TPU:0, one launch (start us, length us, event | category | flops | bytes accessed | tf_op | source)
XLA Modules:
  0.0 269.3 jit_solution(8923908350597091254)
XLA Ops:
  4.2 2.6 collective-permute-start.2
  20.3 2.8 %collective-permute-done.5.refs_6_.refs_9_ = bf16[128,1024]{1,0:T(8,128)(2,1)S(1)} collective-permute-done((bf16[128,1024]{1,0:T(8,128)(2,1)S(1)}, bf16[128,1024]{1,0:T(8,128)(2,1)S(1)}, u32[]{:S(2)}, u32[]{:S(2)}) %collective-permute-start.5) | collective-permute-done | bytes 262176 | tf_op jit(solution)/shard_map/ppermute | solution.py:78
  35.3 3.3 %collective-permute-done.9.refs_4_.refs_7_ = bf16[128,1024]{1,0:T(8,128)(2,1)S(1)} collective-permute-done((bf16[128,1024]{1,0:T(8,128)(2,1)S(1)}, bf16[128,1024]{1,0:T(8,128)(2,1)S(1)}, u32[]{:S(2)}, u32[]{:S(2)}) %collective-permute-start.9) | collective-permute-done | bytes 262176 | tf_op jit(solution)/shard_map/ppermute | solution.py:78
  38.6 2.8 %collective-permute-done.17.refs_6_.refs_9_ = bf16[128,1024]{1,0:T(8,128)(2,1)S(1)} collective-permute-done((bf16[128,1024]{1,0:T(8,128)(2,1)S(1)}, bf16[128,1024]{1,0:T(8,128)(2,1)S(1)}, u32[]{:S(2)}, u32[]{:S(2)}) %collective-permute-start.17) | collective-permute-done | bytes 262176 | tf_op jit(solution)/shard_map/ppermute | solution.py:78
  67.8 2.8 %collective-permute-done.30.refs_4_.refs_7_ = bf16[128,1024]{1,0:T(8,128)(2,1)S(1)} collective-permute-done((bf16[128,1024]{1,0:T(8,128)(2,1)S(1)}, bf16[128,1024]{1,0:T(8,128)(2,1)S(1)}, u32[]{:S(2)}, u32[]{:S(2)}) %collective-permute-start.30) | collective-permute-done | bytes 262176 | tf_op jit(solution)/shard_map/ppermute | solution.py:78
  70.6 2.8 %collective-permute-done.40.refs_6_.refs_9_ = bf16[128,1024]{1,0:T(8,128)(2,1)S(1)} collective-permute-done((bf16[128,1024]{1,0:T(8,128)(2,1)S(1)}, bf16[128,1024]{1,0:T(8,128)(2,1)S(1)}, u32[]{:S(2)}, u32[]{:S(2)}) %collective-permute-start.40) | collective-permute-done | bytes 262176 | tf_op jit(solution)/shard_map/ppermute | solution.py:78
  73.9 12.2 %collective-permute-start.55 = (bf16[128,1024]{1,0:T(8,128)(2,1)S(1)}, bf16[128,1024]{1,0:T(8,128)(2,1)S(1)}, u32[]{:S(2)}, u32[]{:S(2)}) collective-permute-start(bf16[128,1024]{1,0:T(8,128)(2,1)S(1)} %collective-permute-done.30.refs_4_.refs_7_), channel_id=1, source_target_pairs={{0,2},{1,5},{2,6},{3,1},{6,4},{7,3},{4,0},{5,7},{8,10},{9,13},{10,... | collective-permute-start | bytes 786440 | tf_op jit(solution)/shard_map/ppermute | solution.py:78
  91.8 2.6 collective-permute-done.37.refs_4_.refs_7_
  96.9 2.5 collective-permute-done.44.refs_4_.refs_7_
  112.8 4.3 %collective-permute-done.63.got_ref.refs_0_ = bf16[64,1024]{1,0:T(8,128)(2,1)S(1)} collective-permute-done((bf16[64,1024]{1,0:T(8,128)(2,1)S(1)}, bf16[64,1024]{1,0:T(8,128)(2,1)S(1)}, u32[]{:S(2)}, u32[]{:S(2)}) %collective-permute-start.63) | collective-permute-done | bytes 131104 | tf_op jit(solution)/shard_map/ppermute | solution.py:446
  117.1 2.7 collective-permute-start.64
  119.8 2.8 %collective-permute-start.66 = (bf16[64,1024]{1,0:T(8,128)(2,1)S(1)}, bf16[64,1024]{1,0:T(8,128)(2,1)S(1)}, u32[]{:S(2)}, u32[]{:S(2)}) collective-permute-start(bf16[64,1024]{1,0:T(8,128)(2,1)S(1)} %get-tuple-element.237), channel_id=1, source_target_pairs={{0,16},{8,24},{16,0},{24,8},{1,17},{9,25},{17,1},{25,9},{2,18},{10... | collective-permute-start | bytes 393224 | tf_op jit(solution)/shard_map/ppermute | solution.py:454
  122.6 7.0 %collective-permute-done.64.got_ref = bf16[64,1024]{1,0:T(8,128)(2,1)S(1)} collective-permute-done((bf16[64,1024]{1,0:T(8,128)(2,1)S(1)}, bf16[64,1024]{1,0:T(8,128)(2,1)S(1)}, u32[]{:S(2)}, u32[]{:S(2)}) %collective-permute-start.64) | collective-permute-done | bytes 131104 | tf_op jit(solution)/shard_map/ppermute | solution.py:454
  132.1 3.7 %collective-permute-done.67.refs_4_ = bf16[64,1024]{1,0:T(8,128)(2,1)S(1)} collective-permute-done((bf16[64,1024]{1,0:T(8,128)(2,1)S(1)}, bf16[64,1024]{1,0:T(8,128)(2,1)S(1)}, u32[]{:S(2)}, u32[]{:S(2)}) %collective-permute-start.67) | collective-permute-done | bytes 131104 | tf_op jit(solution)/shard_map/ppermute | solution.py:454
  144.0 2.8 %back.12 = (bf16[2,256,4096]{2,1,0:T(8,128)(2,1)}, f32[2,1,4096]{2,1,0:T(1,128)S(1)}, bf16[512,1024]{1,0:T(8,128)(2,1)S(1)}, bf16[512,1024]{1,0:T(8,128)(2,1)S(1)}) custom-call(bf16[256,1024]{1,0:T(8,128)(2,1)S(1)} %get-tuple-element.179.refs_0_, bf16[2,256,4096]{2,1,0:T(8,128)(2,1)S(1)} %copy-done, ...), custom_call_target="tpu_custom_call", output_to_operand_aliasing={{1}: (14, {}), {0}: (15, {})} | custom-call | flops 2952960000 | tf_op jit(solution)/shard_map/back/pallas_call | solution.py:32
  147.4 3.3 %back.13 = (bf16[2,256,4096]{2,1,0:T(8,128)(2,1)}, f32[2,1,4096]{2,1,0:T(1,128)S(1)}, bf16[512,1024]{1,0:T(8,128)(2,1)S(1)}, bf16[512,1024]{1,0:T(8,128)(2,1)S(1)}) custom-call(bf16[256,1024]{1,0:T(8,128)(2,1)S(1)} %get-tuple-element.179.refs_0_, bf16[2,256,4096]{2,1,0:T(8,128)(2,1)S(1)} %copy-done, ...), custom_call_target="tpu_custom_call", output_to_operand_aliasing={{1}: (14, {}), {0}: (15, {})} | custom-call | flops 2952960000 | tf_op jit(solution)/shard_map/back/pallas_call | solution.py:32
  152.1 2.8 %back.14 = (bf16[2,256,4096]{2,1,0:T(8,128)(2,1)}, f32[2,1,4096]{2,1,0:T(1,128)S(1)}, bf16[512,1024]{1,0:T(8,128)(2,1)S(1)}, bf16[512,1024]{1,0:T(8,128)(2,1)S(1)}) custom-call(bf16[256,1024]{1,0:T(8,128)(2,1)S(1)} %get-tuple-element.179.refs_0_, bf16[2,256,4096]{2,1,0:T(8,128)(2,1)S(1)} %copy-done, ...), custom_call_target="tpu_custom_call", output_to_operand_aliasing={{1}: (14, {}), {0}: (15, {})} | custom-call | flops 2952960000 | tf_op jit(solution)/shard_map/back/pallas_call | solution.py:32
  156.3 2.8 %back.15 = (bf16[2,256,4096]{2,1,0:T(8,128)(2,1)}, f32[2,1,4096]{2,1,0:T(1,128)S(1)}, bf16[512,1024]{1,0:T(8,128)(2,1)S(1)}, bf16[512,1024]{1,0:T(8,128)(2,1)S(1)}) custom-call(bf16[256,1024]{1,0:T(8,128)(2,1)S(1)} %get-tuple-element.179.refs_0_, bf16[2,256,4096]{2,1,0:T(8,128)(2,1)S(1)} %copy-done, ...), custom_call_target="tpu_custom_call", output_to_operand_aliasing={{1}: (14, {}), {0}: (15, {})} | custom-call | flops 2952960000 | tf_op jit(solution)/shard_map/back/pallas_call | solution.py:32
  160.6 5.6 %collective-permute-done.75.y_ref = f32[256,1]{1,0:T(8,128)S(1)} collective-permute-done((f32[256,1]{1,0:T(8,128)S(1)}, f32[256,1]{1,0:T(8,128)S(1)}, u32[]{:S(2)}, u32[]{:S(2)}) %collective-permute-start.75) | collective-permute-done | bytes 1056 | tf_op jit(solution)/shard_map/ppermute | solution.py:440
  169.5 3.1 %collective-permute-done.78.refs_4_ = bf16[128,1024]{1,0:T(8,128)(2,1)S(1)} collective-permute-done((bf16[128,1024]{1,0:T(8,128)(2,1)S(1)}, bf16[128,1024]{1,0:T(8,128)(2,1)S(1)}, u32[]{:S(2)}, u32[]{:S(2)}) %collective-permute-start.78) | collective-permute-done | bytes 262176 | tf_op jit(solution)/shard_map/ppermute | solution.py:81
  175.4 2.8 %back.16 = (bf16[2,256,4096]{2,1,0:T(8,128)(2,1)}, f32[2,1,4096]{2,1,0:T(1,128)S(1)}, bf16[512,1024]{1,0:T(8,128)(2,1)S(1)}, bf16[512,1024]{1,0:T(8,128)(2,1)S(1)}) custom-call(bf16[256,1024]{1,0:T(8,128)(2,1)S(1)} %get-tuple-element.179.refs_0_, bf16[2,256,4096]{2,1,0:T(8,128)(2,1)S(1)} %copy-done, ...), custom_call_target="tpu_custom_call", output_to_operand_aliasing={{1}: (14, {}), {0}: (15, {})} | custom-call | flops 2952960000 | tf_op jit(solution)/shard_map/back/pallas_call | solution.py:32
  181.3 2.8 %back.17 = (bf16[2,256,4096]{2,1,0:T(8,128)(2,1)}, f32[2,1,4096]{2,1,0:T(1,128)S(1)}, bf16[512,1024]{1,0:T(8,128)(2,1)S(1)}, bf16[512,1024]{1,0:T(8,128)(2,1)S(1)}) custom-call(bf16[256,1024]{1,0:T(8,128)(2,1)S(1)} %get-tuple-element.179.refs_0_, bf16[2,256,4096]{2,1,0:T(8,128)(2,1)S(1)} %copy-done, ...), custom_call_target="tpu_custom_call", output_to_operand_aliasing={{1}: (14, {}), {0}: (15, {})} | custom-call | flops 2952960000 | tf_op jit(solution)/shard_map/back/pallas_call | solution.py:32
  187.0 4.6 %collective-permute-done.87.refs_7_ = bf16[256,1024]{1,0:T(8,128)(2,1)S(1)} collective-permute-done((bf16[256,1024]{1,0:T(8,128)(2,1)S(1)}, bf16[256,1024]{1,0:T(8,128)(2,1)S(1)}, u32[]{:S(2)}, u32[]{:S(2)}) %collective-permute-start.87) | collective-permute-done | bytes 524320 | tf_op jit(solution)/shard_map/ppermute | solution.py:81
  191.6 5.6 %collective-permute-done.94.refs_7_ = bf16[256,1024]{1,0:T(8,128)(2,1)S(1)} collective-permute-done((bf16[256,1024]{1,0:T(8,128)(2,1)S(1)}, bf16[256,1024]{1,0:T(8,128)(2,1)S(1)}, u32[]{:S(2)}, u32[]{:S(2)}) %collective-permute-start.94) | collective-permute-done | bytes 524320 | tf_op jit(solution)/shard_map/ppermute | solution.py:81
  199.3 7.5 %collective-permute-done.76.y_ref = f32[256,1]{1,0:T(8,128)S(1)} collective-permute-done((f32[256,1]{1,0:T(8,128)S(1)}, f32[256,1]{1,0:T(8,128)S(1)}, u32[]{:S(2)}, u32[]{:S(2)}) %collective-permute-start.76) | collective-permute-done | bytes 1056 | tf_op jit(solution)/shard_map/ppermute | solution.py:440
  217.5 5.0 %collective-permute-done.101.refs_7_ = bf16[256,1024]{1,0:T(8,128)(2,1)S(1)} collective-permute-done((bf16[256,1024]{1,0:T(8,128)(2,1)S(1)}, bf16[256,1024]{1,0:T(8,128)(2,1)S(1)}, u32[]{:S(2)}, u32[]{:S(2)}) %collective-permute-start.101) | collective-permute-done | bytes 524320 | tf_op jit(solution)/shard_map/ppermute | solution.py:81
  223.0 5.1 %collective-permute-done.98.refs_7_ = bf16[256,1024]{1,0:T(8,128)(2,1)S(1)} collective-permute-done((bf16[256,1024]{1,0:T(8,128)(2,1)S(1)}, bf16[256,1024]{1,0:T(8,128)(2,1)S(1)}, u32[]{:S(2)}, u32[]{:S(2)}) %collective-permute-start.98) | collective-permute-done | bytes 524320 | tf_op jit(solution)/shard_map/ppermute | solution.py:81
  234.2 3.0 %collective-permute-done.91.y_ref = f32[2,1,4096]{2,1,0:T(1,128)S(1)} collective-permute-done((f32[2,1,4096]{2,1,0:T(1,128)S(1)}, f32[2,1,4096]{2,1,0:T(1,128)S(1)}, u32[]{:S(2)}, u32[]{:S(2)}) %collective-permute-start.91) | collective-permute-done | bytes 32800 | tf_op jit(solution)/shard_map/ppermute | solution.py:440
  239.9 6.5 %collective-permute-done.108.refs_5_ = bf16[256,1024]{1,0:T(8,128)(2,1)S(1)} collective-permute-done((bf16[256,1024]{1,0:T(8,128)(2,1)S(1)}, bf16[256,1024]{1,0:T(8,128)(2,1)S(1)}, u32[]{:S(2)}, u32[]{:S(2)}) %collective-permute-start.108) | collective-permute-done | bytes 524320 | tf_op jit(solution)/shard_map/ppermute | solution.py:81
  246.4 5.6 %collective-permute-done.105.refs_5_ = bf16[256,1024]{1,0:T(8,128)(2,1)S(1)} collective-permute-done((bf16[256,1024]{1,0:T(8,128)(2,1)S(1)}, bf16[256,1024]{1,0:T(8,128)(2,1)S(1)}, u32[]{:S(2)}, u32[]{:S(2)}) %collective-permute-start.105) | collective-permute-done | bytes 524320 | tf_op jit(solution)/shard_map/ppermute | solution.py:81
  259.9 3.6 %collective-permute-done.112.refs_2_ = bf16[256,512]{1,0:T(8,128)(2,1)S(1)} collective-permute-done((bf16[256,512]{1,0:T(8,128)(2,1)S(1)}, bf16[256,512]{1,0:T(8,128)(2,1)S(1)}, u32[]{:S(2)}, u32[]{:S(2)}) %collective-permute-start.112) | collective-permute-done | bytes 262176 | tf_op jit(solution)/shard_map/ppermute | solution.py:81
  263.5 2.8 %collective-permute-done.110.refs_2_ = bf16[256,512]{1,0:T(8,128)(2,1)S(1)} collective-permute-done((bf16[256,512]{1,0:T(8,128)(2,1)S(1)}, bf16[256,512]{1,0:T(8,128)(2,1)S(1)}, u32[]{:S(2)}, u32[]{:S(2)}) %collective-permute-start.110) | collective-permute-done | bytes 262176 | tf_op jit(solution)/shard_map/ppermute | solution.py:81
  (256 shorter events, 137.7 us)
Async XLA Ops:
  19.5 9.3 %collective-permute-start.6 = (bf16[128,1024]{1,0:T(8,128)(2,1)S(1)}, bf16[128,1024]{1,0:T(8,128)(2,1)S(1)}, u32[]{:S(2)}, u32[]{:S(2)}) collective-permute-start(bf16[128,1024]{1,0:T(8,128)(2,1)S(1)} %collective-permute-done.2.refs_4_.refs_7_), channel_id=1, source_target_pairs={{0,1},{1,0},{2,3},{3,2},{6,7},{7,6},{4,5},{5,4},{8,9},{9,8},{10,11... | collective-permute-start | bytes 786440 | tf_op jit(solution)/shard_map/ppermute | solution.py:84
  23.2 9.0 %collective-permute-start.1 = (bf16[128,1024]{1,0:T(8,128)(2,1)S(1)}, bf16[128,1024]{1,0:T(8,128)(2,1)S(1)}, u32[]{:S(2)}, u32[]{:S(2)}) collective-permute-start(bf16[128,1024]{1,0:T(8,128)(2,1)S(1)} %get-tuple-element.183.refs_3_.refs_6_), channel_id=1, source_target_pairs={{0,2},{1,5},{2,6},{3,1},{6,4},{7,3},{4,0},{5,7},{8,10},{9,13},{10,... | collective-permute-start | bytes 786440 | tf_op jit(solution)/shard_map/ppermute | solution.py:78
  48.3 8.8 %collective-permute-start.39 = (bf16[128,1024]{1,0:T(8,128)(2,1)S(1)}, bf16[128,1024]{1,0:T(8,128)(2,1)S(1)}, u32[]{:S(2)}, u32[]{:S(2)}) collective-permute-start(bf16[128,1024]{1,0:T(8,128)(2,1)S(1)} %collective-permute-done.38.refs_7_.refs_10_), channel_id=1, source_target_pairs={{0,2},{1,5},{2,6},{3,1},{6,4},{7,3},{4,0},{5,7},{8,10},{9,13},{10,... | collective-permute-start | bytes 786440 | tf_op jit(solution)/shard_map/ppermute | solution.py:78
  67.8 20.0 %collective-permute-start.42 = (bf16[128,1024]{1,0:T(8,128)(2,1)S(1)}, bf16[128,1024]{1,0:T(8,128)(2,1)S(1)}, u32[]{:S(2)}, u32[]{:S(2)}) collective-permute-start(bf16[128,1024]{1,0:T(8,128)(2,1)S(1)} %collective-permute-done.39.refs_5_.refs_8_), channel_id=1, source_target_pairs={{0,1},{1,0},{2,3},{3,2},{6,7},{7,6},{4,5},{5,4},{8,9},{9,8},{10,11... | collective-permute-start | bytes 786440 | tf_op jit(solution)/shard_map/ppermute | solution.py:84
  70.6 18.8 %collective-permute-start.41 = (bf16[128,1024]{1,0:T(8,128)(2,1)S(1)}, bf16[128,1024]{1,0:T(8,128)(2,1)S(1)}, u32[]{:S(2)}, u32[]{:S(2)}) collective-permute-start(bf16[128,1024]{1,0:T(8,128)(2,1)S(1)} %collective-permute-done.29.refs_4_.refs_7_), channel_id=1, source_target_pairs={{0,1},{1,0},{2,3},{3,2},{6,7},{7,6},{4,5},{5,4},{8,9},{9,8},{10,11... | collective-permute-start | bytes 786440 | tf_op jit(solution)/shard_map/ppermute | solution.py:84
  73.4 16.0 %collective-permute-start.43 = (bf16[128,1024]{1,0:T(8,128)(2,1)S(1)}, bf16[128,1024]{1,0:T(8,128)(2,1)S(1)}, u32[]{:S(2)}, u32[]{:S(2)}) collective-permute-start(bf16[128,1024]{1,0:T(8,128)(2,1)S(1)} %collective-permute-done.40.refs_6_.refs_9_), channel_id=1, source_target_pairs={{0,1},{1,0},{2,3},{3,2},{6,7},{7,6},{4,5},{5,4},{8,9},{9,8},{10,11... | collective-permute-start | bytes 786440 | tf_op jit(solution)/shard_map/ppermute | solution.py:84
  73.4 22.4 %collective-permute-start.45 = (bf16[128,512]{1,0:T(8,128)(2,1)S(1)}, bf16[128,512]{1,0:T(8,128)(2,1)S(1)}, u32[]{:S(2)}, u32[]{:S(2)}) collective-permute-start(bf16[128,512]{1,0:T(8,128)(2,1)S(1)} %get-tuple-element.216.refs_3_.refs_6_), channel_id=1, source_target_pairs={{0,1},{1,0},{2,3},{3,2},{6,7},{7,6},{4,5},{5,4},{8,9},{9,8},{10,11... | collective-permute-start | bytes 393224 | tf_op jit(solution)/shard_map/ppermute | solution.py:84
  73.9 23.0 %collective-permute-start.55 = (bf16[128,1024]{1,0:T(8,128)(2,1)S(1)}, bf16[128,1024]{1,0:T(8,128)(2,1)S(1)}, u32[]{:S(2)}, u32[]{:S(2)}) collective-permute-start(bf16[128,1024]{1,0:T(8,128)(2,1)S(1)} %collective-permute-done.30.refs_4_.refs_7_), channel_id=1, source_target_pairs={{0,2},{1,5},{2,6},{3,1},{6,4},{7,3},{4,0},{5,7},{8,10},{9,13},{10,... | collective-permute-start | bytes 786440 | tf_op jit(solution)/shard_map/ppermute | solution.py:78
  89.4 10.0 %collective-permute-start.61 = (bf16[128,1024]{1,0:T(8,128)(2,1)S(1)}, bf16[128,1024]{1,0:T(8,128)(2,1)S(1)}, u32[]{:S(2)}, u32[]{:S(2)}) collective-permute-start(bf16[128,1024]{1,0:T(8,128)(2,1)S(1)} %collective-permute-done.48.refs_5_.refs_8_), channel_id=1, source_target_pairs={{0,1},{1,0},{2,3},{3,2},{6,7},{7,6},{4,5},{5,4},{8,9},{9,8},{10,11... | collective-permute-start | bytes 786440 | tf_op jit(solution)/shard_map/ppermute | solution.py:84
  117.1 12.5 %collective-permute-start.64 = (bf16[64,1024]{1,0:T(8,128)(2,1)S(1)}, bf16[64,1024]{1,0:T(8,128)(2,1)S(1)}, u32[]{:S(2)}, u32[]{:S(2)}) collective-permute-start(bf16[64,1024]{1,0:T(8,128)(2,1)S(1)} %get-tuple-element.232), channel_id=1, source_target_pairs={{0,16},{8,24},{16,0},{24,8},{1,17},{9,25},{17,1},{25,9},{2,18},{10... | collective-permute-start | bytes 393224 | tf_op jit(solution)/shard_map/ppermute | solution.py:454
  119.8 11.5 %collective-permute-start.66 = (bf16[64,1024]{1,0:T(8,128)(2,1)S(1)}, bf16[64,1024]{1,0:T(8,128)(2,1)S(1)}, u32[]{:S(2)}, u32[]{:S(2)}) collective-permute-start(bf16[64,1024]{1,0:T(8,128)(2,1)S(1)} %get-tuple-element.237), channel_id=1, source_target_pairs={{0,16},{8,24},{16,0},{24,8},{1,17},{9,25},{17,1},{25,9},{2,18},{10... | collective-permute-start | bytes 393224 | tf_op jit(solution)/shard_map/ppermute | solution.py:454
  146.8 9.4 %collective-permute-start.71 = (bf16[512,1024]{1,0:T(8,128)(2,1)S(1)}, bf16[512,1024]{1,0:T(8,128)(2,1)S(1)}, u32[]{:S(2)}, u32[]{:S(2)}) collective-permute-start(bf16[512,1024]{1,0:T(8,128)(2,1)S(1)} %get-tuple-element.271), channel_id=1, source_target_pairs={{0,1},{1,0},{2,3},{3,2},{6,7},{7,6},{4,5},{5,4},{8,9},{9,8},{10,11... | collective-permute-start | bytes 3145736 | tf_op jit(solution)/shard_map/ppermute | solution.py:84
  150.7 17.1 %collective-permute-start.73 = (bf16[512,1024]{1,0:T(8,128)(2,1)S(1)}, bf16[512,1024]{1,0:T(8,128)(2,1)S(1)}, u32[]{:S(2)}, u32[]{:S(2)}) collective-permute-start(bf16[512,1024]{1,0:T(8,128)(2,1)S(1)} %get-tuple-element.263), channel_id=1, source_target_pairs={{0,1},{1,0},{2,3},{3,2},{6,7},{7,6},{4,5},{5,4},{8,9},{9,8},{10,11... | collective-permute-start | bytes 3145736 | tf_op jit(solution)/shard_map/ppermute | solution.py:84
  155.0 23.2 %collective-permute-start.77 = (bf16[512,1024]{1,0:T(8,128)(2,1)S(1)}, bf16[512,1024]{1,0:T(8,128)(2,1)S(1)}, u32[]{:S(2)}, u32[]{:S(2)}) collective-permute-start(bf16[512,1024]{1,0:T(8,128)(2,1)S(1)} %get-tuple-element.269), channel_id=1, source_target_pairs={{0,1},{1,0},{2,3},{3,2},{6,7},{7,6},{4,5},{5,4},{8,9},{9,8},{10,11... | collective-permute-start | bytes 3145736 | tf_op jit(solution)/shard_map/ppermute | solution.py:84
  159.2 25.6 %collective-permute-start.81 = (bf16[512,1024]{1,0:T(8,128)(2,1)S(1)}, bf16[512,1024]{1,0:T(8,128)(2,1)S(1)}, u32[]{:S(2)}, u32[]{:S(2)}) collective-permute-start(bf16[512,1024]{1,0:T(8,128)(2,1)S(1)} %get-tuple-element.276), channel_id=1, source_target_pairs={{0,1},{1,0},{2,3},{3,2},{6,7},{7,6},{4,5},{5,4},{8,9},{9,8},{10,11... | collective-permute-start | bytes 3145736 | tf_op jit(solution)/shard_map/ppermute | solution.py:84
  168.0 11.6 %collective-permute-start.82 = (bf16[128,1024]{1,0:T(8,128)(2,1)S(1)}, bf16[128,1024]{1,0:T(8,128)(2,1)S(1)}, u32[]{:S(2)}, u32[]{:S(2)}) collective-permute-start(bf16[128,1024]{1,0:T(8,128)(2,1)S(1)} %get-tuple-element.298), channel_id=1, source_target_pairs={{0,4},{1,3},{2,0},{3,7},{6,2},{7,5},{4,6},{5,1},{8,12},{9,11},{10,... | collective-permute-start | bytes 786440 | tf_op jit(solution)/shard_map/ppermute | solution.py:81
  178.2 31.1 %collective-permute-start.85 = (bf16[512,1024]{1,0:T(8,128)(2,1)S(1)}, bf16[512,1024]{1,0:T(8,128)(2,1)S(1)}, u32[]{:S(2)}, u32[]{:S(2)}) collective-permute-start(bf16[512,1024]{1,0:T(8,128)(2,1)S(1)} %get-tuple-element.288), channel_id=1, source_target_pairs={{0,1},{1,0},{2,3},{3,2},{6,7},{7,6},{4,5},{5,4},{8,9},{9,8},{10,11... | collective-permute-start | bytes 3145736 | tf_op jit(solution)/shard_map/ppermute | solution.py:84
  180.3 11.3 %collective-permute-start.87 = (bf16[256,1024]{1,0:T(8,128)(2,1)S(1)}, bf16[256,1024]{1,0:T(8,128)(2,1)S(1)}, u32[]{:S(2)}, u32[]{:S(2)}) collective-permute-start(bf16[256,1024]{1,0:T(8,128)(2,1)S(1)} %get-tuple-element.310), channel_id=1, source_target_pairs={{0,4},{1,3},{2,0},{3,7},{6,2},{7,5},{4,6},{5,1},{8,12},{9,11},{10,... | collective-permute-start | bytes 1572872 | tf_op jit(solution)/shard_map/ppermute | solution.py:81
  184.2 31.5 %collective-permute-start.92 = (bf16[512,1024]{1,0:T(8,128)(2,1)S(1)}, bf16[512,1024]{1,0:T(8,128)(2,1)S(1)}, u32[]{:S(2)}, u32[]{:S(2)}) collective-permute-start(bf16[512,1024]{1,0:T(8,128)(2,1)S(1)} %get-tuple-element.296), channel_id=1, source_target_pairs={{0,1},{1,0},{2,3},{3,2},{6,7},{7,6},{4,5},{5,4},{8,9},{9,8},{10,11... | collective-permute-start | bytes 3145736 | tf_op jit(solution)/shard_map/ppermute | solution.py:84
  186.0 11.2 %collective-permute-start.94 = (bf16[256,1024]{1,0:T(8,128)(2,1)S(1)}, bf16[256,1024]{1,0:T(8,128)(2,1)S(1)}, u32[]{:S(2)}, u32[]{:S(2)}) collective-permute-start(bf16[256,1024]{1,0:T(8,128)(2,1)S(1)} %get-tuple-element.324), channel_id=1, source_target_pairs={{0,4},{1,3},{2,0},{3,7},{6,2},{7,5},{4,6},{5,1},{8,12},{9,11},{10,... | collective-permute-start | bytes 1572872 | tf_op jit(solution)/shard_map/ppermute | solution.py:81
  191.6 17.7 %collective-permute-start.88 = (bf16[256,1024]{1,0:T(8,128)(2,1)S(1)}, bf16[256,1024]{1,0:T(8,128)(2,1)S(1)}, u32[]{:S(2)}, u32[]{:S(2)}) collective-permute-start(bf16[256,1024]{1,0:T(8,128)(2,1)S(1)} %collective-permute-done.87.refs_7_), channel_id=1, source_target_pairs={{0,1},{1,0},{2,3},{3,2},{6,7},{7,6},{4,5},{5,4},{8,9},{9,8},{10,11... | collective-permute-start | bytes 1572872 | tf_op jit(solution)/shard_map/ppermute | solution.py:84
  197.2 18.5 %collective-permute-start.95 = (bf16[256,1024]{1,0:T(8,128)(2,1)S(1)}, bf16[256,1024]{1,0:T(8,128)(2,1)S(1)}, u32[]{:S(2)}, u32[]{:S(2)}) collective-permute-start(bf16[256,1024]{1,0:T(8,128)(2,1)S(1)} %collective-permute-done.94.refs_7_), channel_id=1, source_target_pairs={{0,1},{1,0},{2,3},{3,2},{6,7},{7,6},{4,5},{5,4},{8,9},{9,8},{10,11... | collective-permute-start | bytes 1572872 | tf_op jit(solution)/shard_map/ppermute | solution.py:84
  197.2 9.6 %collective-permute-start.76 = (f32[256,1]{1,0:T(8,128)S(1)}, f32[256,1]{1,0:T(8,128)S(1)}, u32[]{:S(2)}, u32[]{:S(2)}) collective-permute-start(f32[256,1]{1,0:T(8,128)S(1)} %add_two.5.x_ref), channel_id=1, source_target_pairs={{0,16},{8,24},{16,0},{24,8},{1,17},{9,25},{17,1},{25,9},{2,18},{10... | collective-permute-start | bytes 3080 | tf_op jit(solution)/shard_map/ppermute | solution.py:440
  213.3 9.2 %collective-permute-start.101 = (bf16[256,1024]{1,0:T(8,128)(2,1)S(1)}, bf16[256,1024]{1,0:T(8,128)(2,1)S(1)}, u32[]{:S(2)}, u32[]{:S(2)}) collective-permute-start(bf16[256,1024]{1,0:T(8,128)(2,1)S(1)} %get-tuple-element.334), channel_id=1, source_target_pairs={{0,4},{1,3},{2,0},{3,7},{6,2},{7,5},{4,6},{5,1},{8,12},{9,11},{10,... | collective-permute-start | bytes 1572872 | tf_op jit(solution)/shard_map/ppermute | solution.py:81
  216.6 11.5 %collective-permute-start.98 = (bf16[256,1024]{1,0:T(8,128)(2,1)S(1)}, bf16[256,1024]{1,0:T(8,128)(2,1)S(1)}, u32[]{:S(2)}, u32[]{:S(2)}) collective-permute-start(bf16[256,1024]{1,0:T(8,128)(2,1)S(1)} %get-tuple-element.330), channel_id=1, source_target_pairs={{0,4},{1,3},{2,0},{3,7},{6,2},{7,5},{4,6},{5,1},{8,12},{9,11},{10,... | collective-permute-start | bytes 1572872 | tf_op jit(solution)/shard_map/ppermute | solution.py:81
  217.5 13.2 %collective-permute-start.100 = (bf16[512,512]{1,0:T(8,128)(2,1)S(1)}, bf16[512,512]{1,0:T(8,128)(2,1)S(1)}, u32[]{:S(2)}, u32[]{:S(2)}) collective-permute-start(bf16[512,512]{1,0:T(8,128)(2,1)S(1)} %get-tuple-element.306), channel_id=1, source_target_pairs={{0,1},{1,0},{2,3},{3,2},{6,7},{7,6},{4,5},{5,4},{8,9},{9,8},{10,11... | collective-permute-start | bytes 1572872 | tf_op jit(solution)/shard_map/ppermute | solution.py:84
  222.5 9.7 %collective-permute-start.102 = (bf16[256,1024]{1,0:T(8,128)(2,1)S(1)}, bf16[256,1024]{1,0:T(8,128)(2,1)S(1)}, u32[]{:S(2)}, u32[]{:S(2)}) collective-permute-start(bf16[256,1024]{1,0:T(8,128)(2,1)S(1)} %collective-permute-done.101.refs_7_), channel_id=1, source_target_pairs={{0,1},{1,0},{2,3},{3,2},{6,7},{7,6},{4,5},{5,4},{8,9},{9,8},{10,11... | collective-permute-start | bytes 1572872 | tf_op jit(solution)/shard_map/ppermute | solution.py:84
  222.5 14.7 %collective-permute-start.89 = (bf16[512,512]{1,0:T(8,128)(2,1)S(1)}, bf16[512,512]{1,0:T(8,128)(2,1)S(1)}, u32[]{:S(2)}, u32[]{:S(2)}) collective-permute-start(bf16[512,512]{1,0:T(8,128)(2,1)S(1)} %get-tuple-element.317), channel_id=1, source_target_pairs={{0,1},{1,0},{2,3},{3,2},{6,7},{7,6},{4,5},{5,4},{8,9},{9,8},{10,11... | collective-permute-start | bytes 1572872 | tf_op jit(solution)/shard_map/ppermute | solution.py:84
  228.1 9.1 %collective-permute-start.99 = (bf16[256,1024]{1,0:T(8,128)(2,1)S(1)}, bf16[256,1024]{1,0:T(8,128)(2,1)S(1)}, u32[]{:S(2)}, u32[]{:S(2)}) collective-permute-start(bf16[256,1024]{1,0:T(8,128)(2,1)S(1)} %collective-permute-done.98.refs_7_), channel_id=1, source_target_pairs={{0,1},{1,0},{2,3},{3,2},{6,7},{7,6},{4,5},{5,4},{8,9},{9,8},{10,11... | collective-permute-start | bytes 1572872 | tf_op jit(solution)/shard_map/ppermute | solution.py:84
  237.1 9.2 %collective-permute-start.108 = (bf16[256,1024]{1,0:T(8,128)(2,1)S(1)}, bf16[256,1024]{1,0:T(8,128)(2,1)S(1)}, u32[]{:S(2)}, u32[]{:S(2)}) collective-permute-start(bf16[256,1024]{1,0:T(8,128)(2,1)S(1)} %get-tuple-element.345), channel_id=1, source_target_pairs={{0,4},{1,3},{2,0},{3,7},{6,2},{7,5},{4,6},{5,1},{8,12},{9,11},{10,... | collective-permute-start | bytes 1572872 | tf_op jit(solution)/shard_map/ppermute | solution.py:81
  238.5 13.5 %collective-permute-start.105 = (bf16[256,1024]{1,0:T(8,128)(2,1)S(1)}, bf16[256,1024]{1,0:T(8,128)(2,1)S(1)}, u32[]{:S(2)}, u32[]{:S(2)}) collective-permute-start(bf16[256,1024]{1,0:T(8,128)(2,1)S(1)} %get-tuple-element.342), channel_id=1, source_target_pairs={{0,4},{1,3},{2,0},{3,7},{6,2},{7,5},{4,6},{5,1},{8,12},{9,11},{10,... | collective-permute-start | bytes 1572872 | tf_op jit(solution)/shard_map/ppermute | solution.py:81
  246.4 9.8 %collective-permute-start.109 = (bf16[256,1024]{1,0:T(8,128)(2,1)S(1)}, bf16[256,1024]{1,0:T(8,128)(2,1)S(1)}, u32[]{:S(2)}, u32[]{:S(2)}) collective-permute-start(bf16[256,1024]{1,0:T(8,128)(2,1)S(1)} %collective-permute-done.108.refs_5_), channel_id=1, source_target_pairs={{0,1},{1,0},{2,3},{3,2},{6,7},{7,6},{4,5},{5,4},{8,9},{9,8},{10,11... | collective-permute-start | bytes 1572872 | tf_op jit(solution)/shard_map/ppermute | solution.py:84
  (86 other events, 592.6 us)
